TPU v7x, 32 devices: a whole 2x2x4 slice. The times are simulated.
32 devices in a mesh: head: 8 (over y, x, core), ctx: 4 (over z).
Axes of the slice: x: 2, y: 2, z: 4, core: 2. Of those that a mesh axis runs over, the one named last changes fastest.
Arguments:
- queries: bfloat16 [8192, 2048], P(('ctx', 'head')), may hold values from -6 to 6
- keys: bfloat16 [8192, 2048], P(('ctx', 'head')), may hold values from -6 to 6
- values: bfloat16 [8192, 2048], P(('ctx', 'head')), may hold values from -24 to 24
- picks: int32 [16, 2], replicated, may hold values from 0 to 15, as said below
Outputs:
- attended: bfloat16 [8192, 2048], P(('ctx', 'head'))
Inputs may be any that keep to these rules, and one draw needn't show every extreme that they name: `picks`: rows 4 * c to 4 * c + 3 are the query blocks held by index c of ctx, and blocks 4 * o to 4 * o + 3 are held by index o. Among the 8 entries of one such group of rows, at most 3 name blocks held by any one index of ctx; one index o, the same for every group, is named exactly 3 times by every group.
All inputs are finite; a program needn't handle non-finite values.
Results may differ from a plain program's by a relative error of at most 0.0039.
Values may be sent and summed in bfloat16 or wider, within the bound.
No kernel may reach another device: no remote copies, remote signals or barrier semaphores. Data moves between devices by JAX's collectives and lax.ppermute only.
A program may use at most 128 MiB of HBM per device.

v0:
```python
import functools
import math

import jax
import jax.numpy as jnp
from jax import lax
from jax.experimental import pallas as pl
from jax.experimental.pallas import tpu as pltpu
from jax.sharding import PartitionSpec as P

HEADS = 16
HD = 128
BLOCK = 512
RSEL = 2
MAX_STEPS = 8
MIN_STEPS = 6
LATENCY = 2
ANY = pl.ANY


def plan_layout(local_blocks):
    send = 0
    pick = 2 * MAX_STEPS
    ready = pick + local_blocks * RSEL
    steps = ready + local_blocks
    return send, pick, ready, steps, steps + 1


def plan_kernel(groups, local_blocks, me_ref, picks_ref, out_ref):
    rows = max(8, 2 * groups)
    blocks = groups * local_blocks
    lanes = 128 * ((blocks + 127) // 128)
    send, pick, ready, steps, _ = plan_layout(local_blocks)
    f32 = jnp.float32
    lane_i = lax.broadcasted_iota(jnp.int32, (rows, lanes), 1)
    row_i = lax.broadcasted_iota(jnp.int32, (rows, lanes), 0)
    lane = lane_i.astype(f32)
    row = row_i.astype(f32)
    back = row >= groups
    place = jnp.where(back, row - groups, row)
    owner = jnp.zeros((rows, lanes), f32)
    for g in range(1, groups):
        owner = owner + jnp.where(lane_i >= g * local_blocks, 1.0, 0.0)
    origin = jnp.where(back, groups - 1 - owner, owner)
    far = jnp.full((rows, lanes), -1.0, f32)
    for entry in range(blocks * RSEL):
        query = entry // RSEL
        group = query // local_blocks
        named = picks_ref[query, entry % RSEL]
        target = jnp.where(back, f32(groups - 1 - group), f32(group))
        far = jnp.where(lane_i == named, jnp.maximum(far, target), far)
    never = f32(1e6)
    crosses = (far > place) & (origin <= place) & (row_i < 2 * groups)
    rank = (far * groups + (groups - 1 - origin)) * lanes + (lanes - 1 - lane)

    def step(t, carry):
        since, sent, came = carry
        now = t.astype(f32)
        able = crosses & (since <= now) & (sent < 0)
        key = jnp.where(able, rank, -1.0)
        best = jnp.max(key, axis=1, keepdims=True)
        goes = jnp.where(able & (key == best), 1.0, 0.0)
        sent = jnp.where(goes > 0, now, sent)
        lands = pltpu.roll(goes, 1, 0)
        came = jnp.where(lands > 0, now, came)
        since = jnp.where(lands > 0, now + LATENCY, since)
        return since, sent, came

    none = jnp.full((rows, lanes), -1.0, f32)
    held = place == origin
    since, sent, came = lax.fori_loop(0, MAX_STEPS, step, (jnp.where(held, 0.0, never), none, none))
    left = jnp.max(jnp.where(crosses & (sent < 0), 1.0, 0.0))
    last = jnp.max(sent)
    out_ref[steps] = jnp.where(left > 0, MAX_STEPS + 1, last.astype(jnp.int32) + 1)
    me = me_ref[0]
    for way in range(2):
        mine = row_i == (me if way == 0 else 2 * groups - 1 - me)
        source = jnp.where(held, lane - owner * local_blocks, came + local_blocks)
        for t in range(MAX_STEPS):
            code = jnp.sum(jnp.where(mine & (sent == t), source, 0.0))
            out_ref[send + 2 * t + way] = code.astype(jnp.int32)
    for block in range(local_blocks):
        late = jnp.int32(0)
        for slot in range(RSEL):
            named = picks_ref[me * local_blocks + block, slot]
            first = me * local_blocks
            below = named < first
            here = (named >= first) & (named < first + local_blocks)
            watched = jnp.where(below, me, 2 * groups - 1 - me)
            came_at = jnp.sum(jnp.where((row_i == watched) & (lane_i == named), came, 0.0)).astype(jnp.int32)
            code = jnp.where(here, named - first, came_at + local_blocks + jnp.where(below, 0, MAX_STEPS))
            out_ref[pick + block * RSEL + slot] = code
            late = jnp.maximum(late, jnp.where(here, 0, came_at + 1))
        out_ref[ready + block] = late


def make_plan(picks, groups, local_blocks):
    size = plan_layout(local_blocks)[-1]
    me = lax.axis_index("ctx").astype(jnp.int32).reshape(1)
    smem = pl.BlockSpec(memory_space=pltpu.SMEM)
    return pl.pallas_call(
        functools.partial(plan_kernel, groups, local_blocks),
        out_shape=jax.ShapeDtypeStruct((size,), jnp.int32),
        in_specs=[smem, smem],
        out_specs=smem,
        name="plan",
    )(me, picks)


def select_kernel(t, local_blocks, parts, count, after, table_ref, own_ref, *refs):
    came = (refs[:count], refs[count : 2 * count])
    refs = refs[2 * count + after :]
    outs = refs[:2]
    buf, sems = refs[2:]
    for way in range(2):
        code = table_ref[2 * t + way]

        @pl.when(code < local_blocks)
        def _():
            pltpu.make_async_copy(own_ref.at[pl.ds(code * parts, parts)], buf.at[way], sems.at[way]).start()

        for slot in range(count):

            @pl.when(code == local_blocks + slot)
            def _():
                pltpu.make_async_copy(came[way][slot], buf.at[way], sems.at[way]).start()

    for way in range(2):
        pltpu.make_async_copy(own_ref.at[pl.ds(0, parts)], buf.at[way], sems.at[way]).wait()
        pltpu.make_async_copy(buf.at[way], outs[way], sems.at[way]).start()
    for way in range(2):
        pltpu.make_async_copy(buf.at[way], outs[way], sems.at[way]).wait()


def select(t, local_blocks, parts, table, own, came_up, came_down, after):
    count = len(came_up)
    any_spec = pl.BlockSpec(memory_space=ANY)
    shape = jax.ShapeDtypeStruct((parts,) + own.shape[1:], own.dtype)
    return pl.pallas_call(
        functools.partial(select_kernel, t, local_blocks, parts, count, len(after)),
        out_shape=(shape, shape),
        in_specs=[pl.BlockSpec(memory_space=pltpu.SMEM)] + [any_spec] * (1 + 2 * count + len(after)),
        out_specs=(any_spec, any_spec),
        scratch_shapes=[pltpu.VMEM((2,) + shape.shape, shape.dtype), pltpu.SemaphoreType.DMA((2,))],
        compiler_params=pltpu.CompilerParams(vmem_limit_bytes=4 << 20),
        cost_estimate=pl.CostEstimate(flops=0, bytes_accessed=4 << 20, transcendentals=0),
        name="select",
    )(table, own, *came_up, *came_down, *after)


def attend_kernel(low, high, local_blocks, parts, count, chained, table_ref, q_ref, own_ref, *refs):
    came = (refs[:count], refs[count : 2 * count])
    refs = refs[2 * count + (1 if chained else 0) :]
    out_ref, q_buf, kv_buf, o_buf, in_sems, out_sems = refs
    _, pick, ready, _, _ = plan_layout(local_blocks)
    rows = q_ref.shape[1]
    width = q_ref.shape[2]
    heads_here = width // HD
    scale = math.log2(math.e) / math.sqrt(HD)
    slots = RSEL + 1

    def due(block):
        late = table_ref[ready + block]
        return (late > low) & (late <= high) if low >= 0 else late <= high

    def own_part(block):
        return own_ref.at[pl.ds(block * parts, parts)]

    def fetch(block, _):
        @pl.when(due(block))
        def _():
            pltpu.make_async_copy(q_ref.at[pl.ds(block * parts, parts)], q_buf.at[block], in_sems.at[block, slots]).start()
            pltpu.make_async_copy(own_part(block), kv_buf.at[block, 0], in_sems.at[block, 0]).start()
            for slot in range(RSEL):
                code = table_ref[pick + block * RSEL + slot]
                target = kv_buf.at[block, 1 + slot]
                sem = in_sems.at[block, 1 + slot]

                @pl.when(code < local_blocks)
                def _():
                    pltpu.make_async_copy(own_part(code), target, sem).start()

                for way in range(2):
                    for step in range(count):

                        @pl.when(code == local_blocks + way * MAX_STEPS + step)
                        def _():
                            pltpu.make_async_copy(came[way][step], target, sem).start()

        return 0

    def tile(block, part, head):
        cols = pl.ds(pl.multiple_of(head * HD, HD), HD)
        q = q_buf[block, part, :, cols]
        scores = []
        for slot in range(slots):
            for half in range(parts):
                k = kv_buf[block, slot, half, 0, :, cols]
                scores.append(lax.dot_general(q, k, (((1,), (1,)), ((), ())), preferred_element_type=jnp.float32))
        top = functools.reduce(jnp.maximum, [jnp.max(s, axis=1, keepdims=True) for s in scores])
        total = jnp.zeros((rows, HD), jnp.float32)
        mass = jnp.zeros((rows, 1), jnp.float32)
        for index, s in enumerate(scores):
            v = kv_buf[block, index // parts, index % parts, 1, :, cols]
            w = jnp.exp2((s - top) * scale)
            mass = mass + jnp.sum(w, axis=1, keepdims=True)
            total = total + jnp.dot(w.astype(jnp.bfloat16), v, preferred_element_type=jnp.float32)
        o_buf[block, part, :, cols] = (total / mass).astype(jnp.bfloat16)

    def one(block, _):
        @pl.when(due(block))
        def _():
            pltpu.make_async_copy(q_ref.at[pl.ds(0, parts)], q_buf.at[block], in_sems.at[block, slots]).wait()
            for slot in range(slots):
                pltpu.make_async_copy(own_part(0), kv_buf.at[block, slot], in_sems.at[block, slot]).wait()

            def at(i, _):
                tile(block, i // heads_here, i % heads_here)
                return 0

            lax.fori_loop(0, parts * heads_here, at, 0)
            pltpu.make_async_copy(o_buf.at[block], out_ref.at[pl.ds(block * parts, parts)], out_sems.at[block]).start()

        return 0

    def flush(block, _):
        @pl.when(due(block))
        def _():
            pltpu.make_async_copy(o_buf.at[block], out_ref.at[pl.ds(block * parts, parts)], out_sems.at[block]).wait()

        return 0

    lax.fori_loop(0, local_blocks, fetch, 0)
    lax.fori_loop(0, local_blocks, one, 0)
    lax.fori_loop(0, local_blocks, flush, 0)


def attend(low, high, local_blocks, parts, table, q, own, came_up, came_down, so_far):
    count = len(came_up)
    any_spec = pl.BlockSpec(memory_space=ANY)
    chained = so_far is not None
    kv_shape = own.shape[1:]
    inputs = [table, q, own, *came_up, *came_down] + ([so_far] if chained else [])
    return pl.pallas_call(
        functools.partial(attend_kernel, low, high, local_blocks, parts, count, chained),
        out_shape=jax.ShapeDtypeStruct(q.shape, q.dtype),
        in_specs=[pl.BlockSpec(memory_space=pltpu.SMEM)] + [any_spec] * (len(inputs) - 1),
        out_specs=any_spec,
        scratch_shapes=[
            pltpu.VMEM((local_blocks, parts) + q.shape[1:], q.dtype),
            pltpu.VMEM((local_blocks, RSEL + 1, parts) + kv_shape, q.dtype),
            pltpu.VMEM((local_blocks, parts) + q.shape[1:], q.dtype),
            pltpu.SemaphoreType.DMA((local_blocks, RSEL + 2)),
            pltpu.SemaphoreType.DMA((local_blocks,)),
        ],
        input_output_aliases={len(inputs) - 1: 0} if chained else {},
        compiler_params=pltpu.CompilerParams(vmem_limit_bytes=18 << 20),
        cost_estimate=pl.CostEstimate(flops=1 << 30, bytes_accessed=8 << 20, transcendentals=1 << 21),
        name="attend",
    )(*inputs)


def shift(x, by, groups):
    pairs = [(i, i + by) for i in range(groups) if 0 <= i + by < groups]
    return lax.ppermute(x, "ctx", pairs)


def pack_kernel(head_count, *refs):
    ins, out = refs[:-1], refs[-1]
    cols = out.shape[-1]
    for i, ref in enumerate(ins):
        for g in range(head_count):
            out[g, i] = ref[:, g * cols : (g + 1) * cols]


def pack(head_count, *arrays):
    rows, width = arrays[0].shape
    cols = width // head_count
    pieces = 4
    some = rows // pieces
    return pl.pallas_call(
        functools.partial(pack_kernel, head_count),
        grid=(pieces,),
        out_shape=jax.ShapeDtypeStruct((head_count, len(arrays), rows, cols), arrays[0].dtype),
        in_specs=[pl.BlockSpec((some, width), lambda r: (r, 0))] * len(arrays),
        out_specs=pl.BlockSpec((head_count, len(arrays), some, cols), lambda r: (0, 0, r, 0)),
        name="pack",
    )(*arrays)


def swap(x):
    return lax.all_to_all(x, "head", split_axis=0, concat_axis=0, tiled=True)


def hops(steps, groups, local_blocks, parts, q_mine, own, table):
    came_up, came_down = [], []
    q = swap(q_mine)
    out, done = None, -1

    def attend_to(high):
        return attend(done, high, local_blocks, parts, table, q, own, came_up[:high], came_down[:high], out)

    for t in range(steps):
        known = max(0, t + 1 - LATENCY)
        after = [q] if t == LATENCY + 2 else []
        up, down = select(t, local_blocks, parts, table, own, came_up[:known], came_down[:known], after)
        came_up.append(shift(up, 1, groups))
        came_down.append(shift(down, -1, groups))
    for high in (steps - 3, steps - 1, steps):
        out, done = attend_to(high), high
    return swap(out)


def local(queries, keys, values, picks):
    head_count = lax.axis_size("head")
    groups = lax.axis_size("ctx")
    tok_rows, model = queries.shape
    local_blocks = tok_rows * head_count // BLOCK
    parts = BLOCK // tok_rows
    own = swap(pack(head_count, keys, values))
    q_mine = pack(head_count, queries)[:, 0]
    if groups * local_blocks > 16:
        out = by_queries(q_mine, own, picks, groups, local_blocks)
    else:
        table = make_plan(picks, groups, local_blocks)
        order = [MAX_STEPS] + list(range(MIN_STEPS, MAX_STEPS))
        branches = [functools.partial(hops, n, groups, local_blocks, parts) for n in order]
        branches.append(lambda q, kv, tab: by_queries(q, kv, picks, groups, local_blocks))
        steps = table[plan_layout(local_blocks)[3]]
        which = jnp.where(steps == MAX_STEPS, 0, jnp.clip(steps - MIN_STEPS + 1, 1, len(order)))
        out = lax.switch(which, branches, q_mine, own, table)
    return out.transpose(1, 0, 2).reshape(tok_rows, model)


def block_pair(query_block, key_block, value_block):
    scores = jnp.einsum("qhd,khd->hqk", query_block, key_block, preferred_element_type=jnp.float32)
    scores = scores * (1.0 / math.sqrt(HD))
    row_max = jnp.max(scores, axis=-1)
    exponent = jnp.exp(scores - row_max[..., None])
    row_sum = jnp.sum(exponent, axis=-1)
    partial_out = jnp.einsum(
        "hqk,khd->qhd", exponent.astype(jnp.bfloat16), value_block, preferred_element_type=jnp.float32
    )
    return partial_out, row_max, row_sum


def route_tables(picks, local_blocks, ctx_count):
    slots = local_blocks * RSEL
    owners = (picks // local_blocks).reshape(ctx_count, slots)
    within = (picks % local_blocks).reshape(ctx_count, slots)
    owner_ids = jnp.arange(ctx_count, dtype=jnp.int32)
    one_hot = (owners[:, :, None] == owner_ids[None, None, :]).astype(jnp.int32)
    running = jnp.cumsum(one_hot, axis=1)
    position = jnp.sum(one_hot * running, axis=-1) - 1
    return owners, within, position


def by_queries(q_mine, own, picks, ctx_count, local_blocks):
    head_count, tok_rows, width = q_mine.shape
    heads_here = width // HD
    my_index = lax.axis_index("ctx")
    shape = (local_blocks, BLOCK, heads_here, HD)
    q_blocks = swap(q_mine).reshape(shape)
    k_blocks = own[:, 0].reshape(shape)
    v_blocks = own[:, 1].reshape(shape)
    capacity = (local_blocks * RSEL + ctx_count - 1) // ctx_count + 1
    slots = local_blocks * RSEL
    owners, within, position = route_tables(picks, local_blocks, ctx_count)
    mine_owner = lax.dynamic_index_in_dim(owners, my_index, 0, keepdims=False)
    mine_pos = lax.dynamic_index_in_dim(position, my_index, 0, keepdims=False)
    slot_ids = jnp.arange(capacity, dtype=jnp.int32)
    asked = (owners == my_index)[:, :, None] & (position[:, :, None] == slot_ids[None, None, :])
    wanted = jnp.sum(asked.astype(jnp.int32) * within[:, :, None], axis=1)
    pick_back = mine_owner * capacity + mine_pos
    own_out, own_max, own_sum = lax.map(lambda b: block_pair(*b), (q_blocks, k_blocks, v_blocks))
    owner_ids = jnp.arange(ctx_count, dtype=jnp.int32)
    chosen = (mine_owner[:, None, None] == owner_ids[None, :, None]) & (
        mine_pos[:, None, None] == slot_ids[None, None, :]
    )
    query_of_slot = jnp.arange(slots, dtype=jnp.int32) // RSEL
    source_block = jnp.sum(chosen.astype(jnp.int32) * query_of_slot[:, None, None], axis=0)
    arrived = lax.all_to_all(q_blocks[source_block], "ctx", split_axis=0, concat_axis=0, tiled=True)

    def owner_pair(items):
        query_block, block_index = items
        return block_pair(query_block, k_blocks[block_index], v_blocks[block_index])

    far = lax.map(owner_pair, (arrived.reshape((-1,) + shape[1:]), wanted.reshape(-1)))
    back = [
        lax.all_to_all(x.reshape((ctx_count, capacity) + x.shape[1:]), "ctx", split_axis=0, concat_axis=0, tiled=True)
        for x in far
    ]
    back = [x.reshape((-1,) + x.shape[2:])[pick_back] for x in back]
    far_out, far_max, far_sum = [x.reshape((local_blocks, RSEL) + x.shape[1:]) for x in back]
    overall = jnp.maximum(own_max, jnp.max(far_max, axis=1))
    own_factor = jnp.exp(own_max - overall)
    far_factor = jnp.exp(far_max - overall[:, None])
    numer = own_out * jnp.transpose(own_factor, (0, 2, 1))[..., None]
    numer = numer + jnp.sum(far_out * jnp.transpose(far_factor, (0, 1, 3, 2))[..., None], axis=1)
    denom = own_sum * own_factor + jnp.sum(far_sum * far_factor, axis=1)
    result = (numer / jnp.transpose(denom, (0, 2, 1))[..., None]).astype(jnp.bfloat16)
    return swap(result.reshape(head_count, tok_rows, width))


def solution(mesh):
    placed = (P(("ctx", "head"), None), P(("ctx", "head"), None), P(("ctx", "head"), None), P())
    return jax.shard_map(
        local, mesh=mesh, in_specs=placed, out_specs=P(("ctx", "head"), None), check_vma=False
    )
```

profile of v0, /device:TPU:0, one launch (start us, length us, event | category | flops | bytes accessed | tf_op | source)
XLA Modules:
  0.0 135.2 jit_solution(7774072331334051813)
XLA Ops:
  0.0 3.8 %pack.3 = bf16[8,2,256,256]{3,2,1,0:T(8,128)(2,1)} custom-call(bf16[256,2048]{1,0:T(8,128)(2,1)} %refs_0_.3, bf16[256,2048]{1,0:T(8,128)(2,1)} %refs_1_.1), custom_call_target="tpu_custom_call" | custom-call | tf_op jit(solution)/shard_map/pack/pallas_call | solution.py:281
  3.8 5.3 %all-to-all-start.12 = ((bf16[8,2,256,256]{3,2,1,0:T(8,128)(2,1)}), bf16[8,2,256,256]{3,2,1,0:T(8,128)(2,1)S(1)}, u32[]{:S(2)}, u32[]{:S(2)}) async-start(bf16[8,2,256,256]{3,2,1,0:T(8,128)(2,1)} %pack.3), calls=%async_computation.12 | async-start | bytes 4194304 | tf_op jit(solution)/shard_map/all_to_all | solution.py:292
  9.8 2.3 %plan.1 = s32[29]{0:T(128)S(1)} custom-call(s32[1]{0:T(128)} %bitcast.34.me_ref, s32[16,2]{1,0:T(8,128)} %copy.41.picks_ref), custom_call_target="tpu_custom_call" | custom-call | tf_op jit(solution)/shard_map/plan/pallas_call | solution.py:101
  13.9 3.4 %pack.2 = bf16[8,1,256,256]{3,2,1,0:T(8,128)(2,1)} custom-call(bf16[256,2048]{1,0:T(8,128)(2,1)} %refs_0_.2), custom_call_target="tpu_custom_call" | custom-call | tf_op jit(solution)/shard_map/pack/pallas_call | solution.py:281
  17.3 18.4 %all-to-all-done.12 = bf16[8,2,256,256]{3,2,1,0:T(8,128)(2,1)S(1)} async-done(((bf16[8,2,256,256]{3,2,1,0:T(8,128)(2,1)}), bf16[8,2,256,256]{3,2,1,0:T(8,128)(2,1)S(1)}, u32[]{:S(2)}, u32[]{:S(2)}) %all-to-all-start.12) | async-done | bytes 2097184 | tf_op jit(solution)/shard_map/all_to_all | solution.py:292
  35.7 98.3 %conditional.1 = (bf16[8,256,256]{2,1,0:T(8,128)(2,1)S(1)}) conditional(s32[]{:T(128)} %bitcast.35, (bf16[8,256,256]{2,1,0:T(8,128)(2,1)}, s32[29]{0:T(128)S(1)}, bf16[8,2,256,256]{3,2,1,0:T(8,128)(2,1)S(1)}) %tuple.77, (bf16[8,256,256]{2,1,0:T(8,128)(2,1)}, s32[29]{0:T(128)S(1)}, ...), branch_computations={%region_0.1_spmd, %region_1.2_spmd, %region_2.3_spmd, %region_3.19... | conditional | flops 3221225472 | bytes 122684160 | solution.py:331
  35.7 1.6 %select.46 = (bf16[2,2,256,256]{3,2,1,0:T(8,128)(2,1)}, bf16[2,2,256,256]{3,2,1,0:T(8,128)(2,1)}) custom-call(s32[29]{0:T(128)S(1)} %get-tuple-element.113.table_ref, bf16[8,2,256,256]{3,2,1,0:T(8,128)(2,1)S(1)} %get-tuple-element.115.own_ref), custom_call_target="tpu_custom_call" | custom-call | bytes 4194304 | tf_op jit(solution)/shard_map/cond/branch_1_fun/select/pallas_call | solution.py:139
  37.4 3.5 %collective-permute-start.16 = (bf16[2,2,256,256]{3,2,1,0:T(8,128)(2,1)}, bf16[2,2,256,256]{3,2,1,0:T(8,128)(2,1)S(1)}, u32[]{:S(2)}, u32[]{:S(2)}) collective-permute-start(bf16[2,2,256,256]{3,2,1,0:T(8,128)(2,1)} %get-tuple-element.116), channel_id=1, source_target_pairs={{0,1},{1,2},{2,3},{4,5},{5,6},{6,7},{8,9},{9,10},{10,11},{12,13},{... | collective-permute-start | bytes 1572872 | tf_op jit(solution)/shard_map/cond/branch_1_fun/ppermute | solution.py:265
  40.9 1.3 collective-permute-start.18
  42.2 1.7 %select.47 = (bf16[2,2,256,256]{3,2,1,0:T(8,128)(2,1)}, bf16[2,2,256,256]{3,2,1,0:T(8,128)(2,1)}) custom-call(s32[29]{0:T(128)S(1)} %get-tuple-element.113.table_ref, bf16[8,2,256,256]{3,2,1,0:T(8,128)(2,1)S(1)} %get-tuple-element.115.own_ref), custom_call_target="tpu_custom_call" | custom-call | bytes 4194304 | tf_op jit(solution)/shard_map/cond/branch_1_fun/select/pallas_call | solution.py:139
  43.9 4.6 %collective-permute-start.17 = (bf16[2,2,256,256]{3,2,1,0:T(8,128)(2,1)}, bf16[2,2,256,256]{3,2,1,0:T(8,128)(2,1)S(1)}, u32[]{:S(2)}, u32[]{:S(2)}) collective-permute-start(bf16[2,2,256,256]{3,2,1,0:T(8,128)(2,1)} %get-tuple-element.117), channel_id=1, source_target_pairs={{0,1},{1,2},{2,3},{4,5},{5,6},{6,7},{8,9},{9,10},{10,11},{12,13},{... | collective-permute-start | bytes 1572872 | tf_op jit(solution)/shard_map/cond/branch_1_fun/ppermute | solution.py:265
  48.5 1.3 collective-permute-start.20
  49.8 3.6 %all-to-all-start.2 = ((bf16[8,256,256]{2,1,0:T(8,128)(2,1)}), bf16[8,256,256]{2,1,0:T(8,128)(2,1)S(1)}, u32[]{:S(2)}, u32[]{:S(2)}) async-start(bf16[8,256,256]{2,1,0:T(8,128)(2,1)} %get-tuple-element.114), calls=%async_computation.2 | async-start | bytes 2097152 | tf_op jit(solution)/shard_map/cond/branch_1_fun/all_to_all | solution.py:292
  53.5 4.2 %collective-permute-done.18.refs_1_.refs_2_.refs_3_.refs_4_.refs_5_.refs_6_ = bf16[2,2,256,256]{3,2,1,0:T(8,128)(2,1)S(1)} collective-permute-done((bf16[2,2,256,256]{3,2,1,0:T(8,128)(2,1)}, bf16[2,2,256,256]{3,2,1,0:T(8,128)(2,1)S(1)}, u32[]{:S(2)}, u32[]{:S(2)}) %collective-permute-start.18) | collective-permute-done | bytes 524320 | tf_op jit(solution)/shard_map/cond/branch_1_fun/ppermute | solution.py:265
  57.8 2.6 %select.48 = (bf16[2,2,256,256]{3,2,1,0:T(8,128)(2,1)}, bf16[2,2,256,256]{3,2,1,0:T(8,128)(2,1)}) custom-call(s32[29]{0:T(128)S(1)} %get-tuple-element.113.table_ref, bf16[8,2,256,256]{3,2,1,0:T(8,128)(2,1)} %copy-done.3, bf16[2,2,256,256]{3,2,1,0:T(8,128)(2,1)S(1)} %collective-permute-done.16.refs_0_, ...), custom_call_target="tpu_custom_call" | custom-call | bytes 4194304 | tf_op jit(solution)/shard_map/cond/branch_1_fun/select/pallas_call | solution.py:139
  60.3 3.3 %collective-permute-start.19 = (bf16[2,2,256,256]{3,2,1,0:T(8,128)(2,1)}, bf16[2,2,256,256]{3,2,1,0:T(8,128)(2,1)}, u32[]{:S(2)}, u32[]{:S(2)}) collective-permute-start(bf16[2,2,256,256]{3,2,1,0:T(8,128)(2,1)} %get-tuple-element.119), channel_id=1, source_target_pairs={{0,1},{1,2},{2,3},{4,5},{5,6},{6,7},{8,9},{9,10},{10,11},{12,13},{... | collective-permute-start | bytes 1572872 | tf_op jit(solution)/shard_map/cond/branch_1_fun/ppermute | solution.py:265
  63.7 1.3 collective-permute-start.22
  65.0 1.7 %select.49 = (bf16[2,2,256,256]{3,2,1,0:T(8,128)(2,1)}, bf16[2,2,256,256]{3,2,1,0:T(8,128)(2,1)}) custom-call(s32[29]{0:T(128)S(1)} %get-tuple-element.113.table_ref, bf16[8,2,256,256]{3,2,1,0:T(8,128)(2,1)S(1)} %copy-done.4, bf16[2,2,256,256]{3,2,1,0:T(8,128)(2,1)S(1)} %collective-permute-done.16.refs_0_, ...), custom_call_target="tpu_custom_call" | custom-call | bytes 4194304 | tf_op jit(solution)/shard_map/cond/branch_1_fun/select/pallas_call | solution.py:139
  66.6 5.4 %collective-permute-start.21 = (bf16[2,2,256,256]{3,2,1,0:T(8,128)(2,1)}, bf16[2,2,256,256]{3,2,1,0:T(8,128)(2,1)}, u32[]{:S(2)}, u32[]{:S(2)}) collective-permute-start(bf16[2,2,256,256]{3,2,1,0:T(8,128)(2,1)} %get-tuple-element.121), channel_id=1, source_target_pairs={{0,1},{1,2},{2,3},{4,5},{5,6},{6,7},{8,9},{9,10},{10,11},{12,13},{... | collective-permute-start | bytes 1572872 | tf_op jit(solution)/shard_map/cond/branch_1_fun/ppermute | solution.py:265
  72.0 1.3 collective-permute-start.24
  73.3 2.2 %collective-permute-done.19.refs_2_ = bf16[2,2,256,256]{3,2,1,0:T(8,128)(2,1)} collective-permute-done((bf16[2,2,256,256]{3,2,1,0:T(8,128)(2,1)}, bf16[2,2,256,256]{3,2,1,0:T(8,128)(2,1)}, u32[]{:S(2)}, u32[]{:S(2)}) %collective-permute-start.19) | collective-permute-done | bytes 524320 | tf_op jit(solution)/shard_map/cond/branch_1_fun/ppermute | solution.py:265
  75.5 4.3 %collective-permute-done.22.refs_5_.refs_6_.refs_7_.refs_8_ = bf16[2,2,256,256]{3,2,1,0:T(8,128)(2,1)} collective-permute-done((bf16[2,2,256,256]{3,2,1,0:T(8,128)(2,1)}, bf16[2,2,256,256]{3,2,1,0:T(8,128)(2,1)}, u32[]{:S(2)}, u32[]{:S(2)}) %collective-permute-start.22) | collective-permute-done | bytes 524320 | tf_op jit(solution)/shard_map/cond/branch_1_fun/ppermute | solution.py:265
  79.8 1.8 %select.50 = (bf16[2,2,256,256]{3,2,1,0:T(8,128)(2,1)S(1)}, bf16[2,2,256,256]{3,2,1,0:T(8,128)(2,1)S(1)}) custom-call(s32[29]{0:T(128)S(1)} %get-tuple-element.113.table_ref, bf16[8,2,256,256]{3,2,1,0:T(8,128)(2,1)} %copy-done.3, bf16[2,2,256,256]{3,2,1,0:T(8,128)(2,1)S(1)} %collective-permute-done.16.refs_0_, ...), custom_call_target="tpu_custom_call" | custom-call | bytes 4194304 | tf_op jit(solution)/shard_map/cond/branch_1_fun/select/pallas_call | solution.py:139
  81.6 3.6 %collective-permute-start.23 = (bf16[2,2,256,256]{3,2,1,0:T(8,128)(2,1)S(1)}, bf16[2,2,256,256]{3,2,1,0:T(8,128)(2,1)S(1)}, u32[]{:S(2)}, u32[]{:S(2)}) collective-permute-start(bf16[2,2,256,256]{3,2,1,0:T(8,128)(2,1)S(1)} %get-tuple-element.123), channel_id=1, source_target_pairs={{0,1},{1,2},{2,3},{4,5},{5,6},{6,7},{8,9},{9,10},{10,11},{12,13},{... | collective-permute-start | bytes 1572872 | tf_op jit(solution)/shard_map/cond/branch_1_fun/ppermute | solution.py:265
  85.3 1.3 collective-permute-start.26
  86.8 4.3 %collective-permute-done.24.refs_7_.refs_8_.refs_9_ = bf16[2,2,256,256]{3,2,1,0:T(8,128)(2,1)} collective-permute-done((bf16[2,2,256,256]{3,2,1,0:T(8,128)(2,1)}, bf16[2,2,256,256]{3,2,1,0:T(8,128)(2,1)}, u32[]{:S(2)}, u32[]{:S(2)}) %collective-permute-start.24) | collective-permute-done | bytes 524320 | tf_op jit(solution)/shard_map/cond/branch_1_fun/ppermute | solution.py:265
  91.8 4.6 %collective-permute-start.25 = (bf16[2,2,256,256]{3,2,1,0:T(8,128)(2,1)S(1)}, bf16[2,2,256,256]{3,2,1,0:T(8,128)(2,1)S(1)}, u32[]{:S(2)}, u32[]{:S(2)}) collective-permute-start(bf16[2,2,256,256]{3,2,1,0:T(8,128)(2,1)S(1)} %get-tuple-element.125), channel_id=1, source_target_pairs={{0,1},{1,2},{2,3},{4,5},{5,6},{6,7},{8,9},{9,10},{10,11},{12,13},{... | collective-permute-start | bytes 1572872 | tf_op jit(solution)/shard_map/cond/branch_1_fun/ppermute | solution.py:265
  96.4 1.5 %collective-permute-start.27 = (bf16[2,2,256,256]{3,2,1,0:T(8,128)(2,1)S(1)}, bf16[2,2,256,256]{3,2,1,0:T(8,128)(2,1)S(1)}, u32[]{:S(2)}, u32[]{:S(2)}) collective-permute-start(bf16[2,2,256,256]{3,2,1,0:T(8,128)(2,1)S(1)} %get-tuple-element.127), channel_id=1, source_target_pairs={{1,0},{2,1},{3,2},{5,4},{6,5},{7,6},{9,8},{10,9},{11,10},{13,12},{... | collective-permute-start | bytes 1572872 | tf_op jit(solution)/shard_map/cond/branch_1_fun/ppermute | solution.py:265
  97.9 4.3 %attend.12.refs_10_ = bf16[8,256,256]{2,1,0:T(8,128)(2,1)S(1)} custom-call(s32[29]{0:T(128)S(1)} %get-tuple-element.113.table_ref, bf16[8,256,256]{2,1,0:T(8,128)(2,1)S(1)} %all-to-all-done.2.refs_6_.q_ref, bf16[8,2,256,256]{3,2,1,0:T(8,128)(2,1)S(1)} %copy-done.5, bf16[2,2,256,256]{3,2,1,0:T(8,128)(2,1)S(1)} %collective-permute-done.16.refs_0_, ...), custom_call_target="tpu_custom_call" | custom-call | flops 1073741824 | bytes 8388608 | tf_op jit(solution)/shard_map/cond/branch_1_fun/attend/pallas_call | solution.py:244
  102.2 7.6 %attend.13.refs_12_ = bf16[8,256,256]{2,1,0:T(8,128)(2,1)S(1)} custom-call(s32[29]{0:T(128)S(1)} %get-tuple-element.113.table_ref, bf16[8,256,256]{2,1,0:T(8,128)(2,1)S(1)} %all-to-all-done.2.refs_6_.q_ref, bf16[8,2,256,256]{3,2,1,0:T(8,128)(2,1)S(1)} %copy-done.5, ...), custom_call_target="tpu_custom_call", output_to_operand_aliasing={{}: (13, {})} | custom-call | flops 1073741824 | bytes 8388608 | tf_op jit(solution)/shard_map/cond/branch_1_fun/attend/pallas_call | solution.py:244
  110.1 4.3 %attend.14 = bf16[8,256,256]{2,1,0:T(8,128)(2,1)S(1)} custom-call(s32[29]{0:T(128)S(1)} %get-tuple-element.113.table_ref, bf16[8,256,256]{2,1,0:T(8,128)(2,1)S(1)} %all-to-all-done.2.refs_6_.q_ref, bf16[8,2,256,256]{3,2,1,0:T(8,128)(2,1)S(1)} %copy-done.5, ...), custom_call_target="tpu_custom_call", output_to_operand_aliasing={{}: (15, {})} | custom-call | flops 1073741824 | bytes 8388608 | tf_op jit(solution)/shard_map/cond/branch_1_fun/attend/pallas_call | solution.py:244
  114.4 19.7 %all_to_all.54 = bf16[8,256,256]{2,1,0:T(8,128)(2,1)S(1)} all-to-all(bf16[8,256,256]{2,1,0:T(8,128)(2,1)S(1)} %attend.14), channel_id=1, replica_groups=mesh['head'=8,'ctx'=4] {'head'}, dimensions={0} | all-to-all | bytes 2097152 | tf_op jit(solution)/shard_map/cond/branch_1_fun/all_to_all | solution.py:292
  (21 shorter events, 3.8 us)
Async XLA Ops:
  3.8 5.3 %copy-start.10 = (s32[16,2]{0,1:T(2,128)S(1)}, s32[16,2]{0,1:T(2,128)}, u32[]{:S(2)}) copy-start(s32[16,2]{0,1:T(2,128)} %param.15) | copy-start | bytes 388
  3.8 31.9 %all-to-all-start.12 = ((bf16[8,2,256,256]{3,2,1,0:T(8,128)(2,1)}), bf16[8,2,256,256]{3,2,1,0:T(8,128)(2,1)S(1)}, u32[]{:S(2)}, u32[]{:S(2)}) async-start(bf16[8,2,256,256]{3,2,1,0:T(8,128)(2,1)} %pack.3), calls=%async_computation.12 | async-start | bytes 4194304 | tf_op jit(solution)/shard_map/all_to_all | solution.py:292
  35.7 8.1 %copy-start.3 = (bf16[8,2,256,256]{3,2,1,0:T(8,128)(2,1)}, bf16[8,2,256,256]{3,2,1,0:T(8,128)(2,1)S(1)}, u32[]{:S(2)}) copy-start(bf16[8,2,256,256]{3,2,1,0:T(8,128)(2,1)S(1)} %get-tuple-element.115.own_ref) | copy-start | bytes 6291460 | tf_op jit(solution)/shard_map/cond
  37.4 16.2 %collective-permute-start.16 = (bf16[2,2,256,256]{3,2,1,0:T(8,128)(2,1)}, bf16[2,2,256,256]{3,2,1,0:T(8,128)(2,1)S(1)}, u32[]{:S(2)}, u32[]{:S(2)}) collective-permute-start(bf16[2,2,256,256]{3,2,1,0:T(8,128)(2,1)} %get-tuple-element.116), channel_id=1, source_target_pairs={{0,1},{1,2},{2,3},{4,5},{5,6},{6,7},{8,9},{9,10},{10,11},{12,13},{... | collective-permute-start | bytes 1572872 | tf_op jit(solution)/shard_map/cond/branch_1_fun/ppermute | solution.py:265
  40.9 16.9 %collective-permute-start.18 = (bf16[2,2,256,256]{3,2,1,0:T(8,128)(2,1)}, bf16[2,2,256,256]{3,2,1,0:T(8,128)(2,1)S(1)}, u32[]{:S(2)}, u32[]{:S(2)}) collective-permute-start(bf16[2,2,256,256]{3,2,1,0:T(8,128)(2,1)} %get-tuple-element.118), channel_id=1, source_target_pairs={{1,0},{2,1},{3,2},{5,4},{6,5},{7,6},{9,8},{10,9},{11,10},{13,12},{... | collective-permute-start | bytes 1572872 | tf_op jit(solution)/shard_map/cond/branch_1_fun/ppermute | solution.py:265
  43.9 21.1 %collective-permute-start.17 = (bf16[2,2,256,256]{3,2,1,0:T(8,128)(2,1)}, bf16[2,2,256,256]{3,2,1,0:T(8,128)(2,1)S(1)}, u32[]{:S(2)}, u32[]{:S(2)}) collective-permute-start(bf16[2,2,256,256]{3,2,1,0:T(8,128)(2,1)} %get-tuple-element.117), channel_id=1, source_target_pairs={{0,1},{1,2},{2,3},{4,5},{5,6},{6,7},{8,9},{9,10},{10,11},{12,13},{... | collective-permute-start | bytes 1572872 | tf_op jit(solution)/shard_map/cond/branch_1_fun/ppermute | solution.py:265
  48.5 16.5 %collective-permute-start.20 = (bf16[2,2,256,256]{3,2,1,0:T(8,128)(2,1)}, bf16[2,2,256,256]{3,2,1,0:T(8,128)(2,1)S(1)}, u32[]{:S(2)}, u32[]{:S(2)}) collective-permute-start(bf16[2,2,256,256]{3,2,1,0:T(8,128)(2,1)} %get-tuple-element.120), channel_id=1, source_target_pairs={{1,0},{2,1},{3,2},{5,4},{6,5},{7,6},{9,8},{10,9},{11,10},{13,12},{... | collective-permute-start | bytes 1572872 | tf_op jit(solution)/shard_map/cond/branch_1_fun/ppermute | solution.py:265
  49.8 23.6 %all-to-all-start.2 = ((bf16[8,256,256]{2,1,0:T(8,128)(2,1)}), bf16[8,256,256]{2,1,0:T(8,128)(2,1)S(1)}, u32[]{:S(2)}, u32[]{:S(2)}) async-start(bf16[8,256,256]{2,1,0:T(8,128)(2,1)} %get-tuple-element.114), calls=%async_computation.2 | async-start | bytes 2097152 | tf_op jit(solution)/shard_map/cond/branch_1_fun/all_to_all | solution.py:292
  53.3 11.6 %copy-start.4 = (bf16[8,2,256,256]{3,2,1,0:T(8,128)(2,1)S(1)}, bf16[8,2,256,256]{3,2,1,0:T(8,128)(2,1)}, u32[]{:S(2)}) copy-start(bf16[8,2,256,256]{3,2,1,0:T(8,128)(2,1)} %copy-done.3) | copy-start | bytes 6291460 | tf_op jit(solution)/shard_map/cond
  60.3 15.2 %collective-permute-start.19 = (bf16[2,2,256,256]{3,2,1,0:T(8,128)(2,1)}, bf16[2,2,256,256]{3,2,1,0:T(8,128)(2,1)}, u32[]{:S(2)}, u32[]{:S(2)}) collective-permute-start(bf16[2,2,256,256]{3,2,1,0:T(8,128)(2,1)} %get-tuple-element.119), channel_id=1, source_target_pairs={{0,1},{1,2},{2,3},{4,5},{5,6},{6,7},{8,9},{9,10},{10,11},{12,13},{... | collective-permute-start | bytes 1572872 | tf_op jit(solution)/shard_map/cond/branch_1_fun/ppermute | solution.py:265
  63.7 16.2 %collective-permute-start.22 = (bf16[2,2,256,256]{3,2,1,0:T(8,128)(2,1)}, bf16[2,2,256,256]{3,2,1,0:T(8,128)(2,1)}, u32[]{:S(2)}, u32[]{:S(2)}) collective-permute-start(bf16[2,2,256,256]{3,2,1,0:T(8,128)(2,1)} %get-tuple-element.122), channel_id=1, source_target_pairs={{1,0},{2,1},{3,2},{5,4},{6,5},{7,6},{9,8},{10,9},{11,10},{13,12},{... | collective-permute-start | bytes 1572872 | tf_op jit(solution)/shard_map/cond/branch_1_fun/ppermute | solution.py:265
  66.6 20.1 %collective-permute-start.21 = (bf16[2,2,256,256]{3,2,1,0:T(8,128)(2,1)}, bf16[2,2,256,256]{3,2,1,0:T(8,128)(2,1)}, u32[]{:S(2)}, u32[]{:S(2)}) collective-permute-start(bf16[2,2,256,256]{3,2,1,0:T(8,128)(2,1)} %get-tuple-element.121), channel_id=1, source_target_pairs={{0,1},{1,2},{2,3},{4,5},{5,6},{6,7},{8,9},{9,10},{10,11},{12,13},{... | collective-permute-start | bytes 1572872 | tf_op jit(solution)/shard_map/cond/branch_1_fun/ppermute | solution.py:265
  72.0 19.0 %collective-permute-start.24 = (bf16[2,2,256,256]{3,2,1,0:T(8,128)(2,1)}, bf16[2,2,256,256]{3,2,1,0:T(8,128)(2,1)}, u32[]{:S(2)}, u32[]{:S(2)}) collective-permute-start(bf16[2,2,256,256]{3,2,1,0:T(8,128)(2,1)} %get-tuple-element.124), channel_id=1, source_target_pairs={{1,0},{2,1},{3,2},{5,4},{6,5},{7,6},{9,8},{10,9},{11,10},{13,12},{... | collective-permute-start | bytes 1572872 | tf_op jit(solution)/shard_map/cond/branch_1_fun/ppermute | solution.py:265
  73.3 17.8 %copy-start.5 = (bf16[8,2,256,256]{3,2,1,0:T(8,128)(2,1)S(1)}, bf16[8,2,256,256]{3,2,1,0:T(8,128)(2,1)}, u32[]{:S(2)}) copy-start(bf16[8,2,256,256]{3,2,1,0:T(8,128)(2,1)} %copy-done.3) | copy-start | bytes 6291460 | tf_op jit(solution)/shard_map/cond
  81.6 20.5 %collective-permute-start.23 = (bf16[2,2,256,256]{3,2,1,0:T(8,128)(2,1)S(1)}, bf16[2,2,256,256]{3,2,1,0:T(8,128)(2,1)S(1)}, u32[]{:S(2)}, u32[]{:S(2)}) collective-permute-start(bf16[2,2,256,256]{3,2,1,0:T(8,128)(2,1)S(1)} %get-tuple-element.123), channel_id=1, source_target_pairs={{0,1},{1,2},{2,3},{4,5},{5,6},{6,7},{8,9},{9,10},{10,11},{12,13},{... | collective-permute-start | bytes 1572872 | tf_op jit(solution)/shard_map/cond/branch_1_fun/ppermute | solution.py:265
  85.3 16.9 %collective-permute-start.26 = (bf16[2,2,256,256]{3,2,1,0:T(8,128)(2,1)S(1)}, bf16[2,2,256,256]{3,2,1,0:T(8,128)(2,1)S(1)}, u32[]{:S(2)}, u32[]{:S(2)}) collective-permute-start(bf16[2,2,256,256]{3,2,1,0:T(8,128)(2,1)S(1)} %get-tuple-element.126), channel_id=1, source_target_pairs={{1,0},{2,1},{3,2},{5,4},{6,5},{7,6},{9,8},{10,9},{11,10},{13,12},{... | collective-permute-start | bytes 1572872 | tf_op jit(solution)/shard_map/cond/branch_1_fun/ppermute | solution.py:265
  91.8 18.0 %collective-permute-start.25 = (bf16[2,2,256,256]{3,2,1,0:T(8,128)(2,1)S(1)}, bf16[2,2,256,256]{3,2,1,0:T(8,128)(2,1)S(1)}, u32[]{:S(2)}, u32[]{:S(2)}) collective-permute-start(bf16[2,2,256,256]{3,2,1,0:T(8,128)(2,1)S(1)} %get-tuple-element.125), channel_id=1, source_target_pairs={{0,1},{1,2},{2,3},{4,5},{5,6},{6,7},{8,9},{9,10},{10,11},{12,13},{... | collective-permute-start | bytes 1572872 | tf_op jit(solution)/shard_map/cond/branch_1_fun/ppermute | solution.py:265
  96.4 13.7 %collective-permute-start.27 = (bf16[2,2,256,256]{3,2,1,0:T(8,128)(2,1)S(1)}, bf16[2,2,256,256]{3,2,1,0:T(8,128)(2,1)S(1)}, u32[]{:S(2)}, u32[]{:S(2)}) collective-permute-start(bf16[2,2,256,256]{3,2,1,0:T(8,128)(2,1)S(1)} %get-tuple-element.127), channel_id=1, source_target_pairs={{1,0},{2,1},{3,2},{5,4},{6,5},{7,6},{9,8},{10,9},{11,10},{13,12},{... | collective-permute-start | bytes 1572872 | tf_op jit(solution)/shard_map/cond/branch_1_fun/ppermute | solution.py:265
where the time goes:
time: 136 us; the launch traced here: 135 us
  starting transfers between devices  41.7 us (31%)
  Pallas kernels  35.7 us (26%)
  waiting for transfers between devices  34.1 us (25%)
  blocking collectives  19.7 us (14%)
  local copies, waits for them, and re-layouts  2.38 us (2%)
    ppermute x12, starting transfers between devices, shift(): return lax.ppermute(x, 'ctx', pairs)  32.9 us
    all_to_all x1, blocking collectives, swap(): return lax.all_to_all(x, 'head', split_axis=0, concat_axis=0, tiled=True)  19.7 us
    all_to_all x2, waiting for transfers between devices, swap(): return lax.all_to_all(x, 'head', split_axis=0, concat_axis=0, tiled=True)  18.4 us
    pallas_call x3, Pallas kernels, attend(): pl.pallas_call(functools.partial(attend_kernel, low, high, local_blocks,...  16.2 us
    ppermute x12, waiting for transfers between devices, shift(): return lax.ppermute(x, 'ctx', pairs)  15.7 us
    pallas_call x6, Pallas kernels, select(): pl.pallas_call(functools.partial(select_kernel, t, local_blocks, parts, c...  10.1 us
    all_to_all x2, starting transfers between devices, swap(): return lax.all_to_all(x, 'head', split_axis=0, concat_axis=0, tiled=True)  8.87 us
    pallas_call x2, Pallas kernels, pack(): pl.pallas_call(functools.partial(pack_kernel, head_count), grid=(pieces,)...  7.13 us
  transfers between devices with their start and end apart: 14, of which 8 were waited for; matrix products, arithmetic and copies ran while one was open for 1% of the time, Pallas kernels for 19%

commit v1 on v0

--- a/solution.py
+++ b/solution.py
@@ -266,24 +266,41 @@
 
 
 def pack_kernel(head_count, *refs):
-    ins, out = refs[:-1], refs[-1]
+    ins, (out, buf, in_sems, out_sems) = refs[:-4], refs[-4:]
     cols = out.shape[-1]
-    for i, ref in enumerate(ins):
-        for g in range(head_count):
-            out[g, i] = ref[:, g * cols : (g + 1) * cols]
+
+    def come(g, i):
+        return pltpu.make_async_copy(ins[i].at[:, pl.ds(g * cols, cols)], buf.at[g, i], in_sems.at[g, i])
+
+    def go(g):
+        return pltpu.make_async_copy(buf.at[g], out.at[g], out_sems.at[g])
+
+    for g in range(head_count):
+        for i in range(len(ins)):
+            come(g, i).start()
+    for g in range(head_count):
+        for i in range(len(ins)):
+            come(g, i).wait()
+        go(g).start()
+    for g in range(head_count):
+        go(g).wait()
 
 
 def pack(head_count, *arrays):
     rows, width = arrays[0].shape
-    cols = width // head_count
-    pieces = 4
-    some = rows // pieces
+    shape = (head_count, len(arrays), rows, width // head_count)
+    any_spec = pl.BlockSpec(memory_space=ANY)
     return pl.pallas_call(
         functools.partial(pack_kernel, head_count),
-        grid=(pieces,),
-        out_shape=jax.ShapeDtypeStruct((head_count, len(arrays), rows, cols), arrays[0].dtype),
-        in_specs=[pl.BlockSpec((some, width), lambda r: (r, 0))] * len(arrays),
-        out_specs=pl.BlockSpec((head_count, len(arrays), some, cols), lambda r: (0, 0, r, 0)),
+        out_shape=jax.ShapeDtypeStruct(shape, arrays[0].dtype),
+        in_specs=[any_spec] * len(arrays),
+        out_specs=any_spec,
+        scratch_shapes=[
+            pltpu.VMEM(shape, arrays[0].dtype),
+            pltpu.SemaphoreType.DMA((head_count, len(arrays))),
+            pltpu.SemaphoreType.DMA((head_count,)),
+        ],
+        compiler_params=pltpu.CompilerParams(vmem_limit_bytes=8 << 20),
         name="pack",
     )(*arrays)
 

time: 136 us -> 149 us (1.096)
  waiting for transfers between devices: 34.1 us -> 45.3 us
  starting transfers between devices: 41.7 us -> 46.1 us
  Pallas kernels: 35.7 us -> 32.5 us
  local copies, waits for them, and re-layouts: 2.38 us -> 4.83 us
    ppermute x12 -> x14, waiting for transfers between devices: 15.7 us -> 24.7 us  [shift(): return lax.ppermute(x, 'ctx', pairs)]
    ppermute x12 -> x14, starting transfers between devices: 32.9 us -> 37.3 us  [shift(): return lax.ppermute(x, 'ctx', pairs)]
    pallas_call x2, Pallas kernels: 7.13 us -> 3.08 us  [pack(): pl.pallas_call(functools.partial(pack_kernel, head_count), out_shape=jax....]
    unnamed x3 -> x9, local copies, waits for them, and re-layouts: 0.68 us -> 3.14 us
    all_to_all x2, waiting for transfers between devices: 18.4 us -> 20.5 us  [swap(): return lax.all_to_all(x, 'head', split_axis=0, concat_axis=0, tiled=True)]
    pallas_call x6 -> x7, Pallas kernels: 10.1 us -> 10.1 us  [select(): pl.pallas_call(functools.partial(select_kernel, t, local_blocks, parts, c...]
  transfers between devices with their start and end apart: 14 -> 16, of which waited for: 8 -> 10; matrix products, arithmetic and copies ran while one was open for 1% -> 1% of each run, Pallas kernels for 19% -> 17%
where the time goes in v1:
time: 149 us
  starting transfers between devices  46.1 us (31%)
  waiting for transfers between devices  45.3 us (30%)
  Pallas kernels  32.5 us (22%)
  blocking collectives  19 us (13%)
  local copies, waits for them, and re-layouts  4.83 us (3%)
    ppermute x14, starting transfers between devices, shift(): return lax.ppermute(x, 'ctx', pairs)  37.3 us
    ppermute x14, waiting for transfers between devices, shift(): return lax.ppermute(x, 'ctx', pairs)  24.7 us
    all_to_all x2, waiting for transfers between devices, swap(): return lax.all_to_all(x, 'head', split_axis=0, concat_axis=0, tiled=True)  20.5 us
    all_to_all x1, blocking collectives, swap(): return lax.all_to_all(x, 'head', split_axis=0, concat_axis=0, tiled=True)  19 us
    pallas_call x3, Pallas kernels, attend(): pl.pallas_call(functools.partial(attend_kernel, low, high, local_blocks,...  17 us
    pallas_call x7, Pallas kernels, select(): pl.pallas_call(functools.partial(select_kernel, t, local_blocks, parts, c...  10.1 us
    all_to_all x2, starting transfers between devices, swap(): return lax.all_to_all(x, 'head', split_axis=0, concat_axis=0, tiled=True)  8.89 us
    unnamed x9, local copies, waits for them, and re-layouts  3.14 us
  transfers between devices with their start and end apart: 16, of which 10 were waited for; matrix products, arithmetic and copies ran while one was open for 1% of the time, Pallas kernels for 17%

profile of v1, /device:TPU:0, one launch (start us, length us, event | category | flops | bytes accessed | tf_op | source)
XLA Modules:
  0.0 149.3 jit_solution(12777078105671863601)
XLA Ops:
  2.5 1.8 %pack.3 = bf16[8,2,256,256]{3,2,1,0:T(8,128)(2,1)} custom-call(bf16[256,2048]{1,0:T(8,128)(2,1)S(1)} %copy-done.1, bf16[256,2048]{1,0:T(8,128)(2,1)S(1)} %copy-done.2), custom_call_target="tpu_custom_call" | custom-call | tf_op jit(solution)/shard_map/pack/pallas_call | solution.py:293
  4.3 5.3 %all-to-all-start.12 = ((bf16[8,2,256,256]{3,2,1,0:T(8,128)(2,1)}), bf16[8,2,256,256]{3,2,1,0:T(8,128)(2,1)S(1)}, u32[]{:S(2)}, u32[]{:S(2)}) async-start(bf16[8,2,256,256]{3,2,1,0:T(8,128)(2,1)} %pack.3), calls=%async_computation.12 | async-start | bytes 4194304 | tf_op jit(solution)/shard_map/all_to_all | solution.py:309
  10.3 2.3 %plan.1 = s32[29]{0:T(128)S(1)} custom-call(s32[1]{0:T(128)} %bitcast.34.me_ref, s32[16,2]{1,0:T(8,128)} %copy.41.picks_ref), custom_call_target="tpu_custom_call" | custom-call | tf_op jit(solution)/shard_map/plan/pallas_call | solution.py:101
  15.8 20.5 %all-to-all-done.12 = bf16[8,2,256,256]{3,2,1,0:T(8,128)(2,1)S(1)} async-done(((bf16[8,2,256,256]{3,2,1,0:T(8,128)(2,1)}), bf16[8,2,256,256]{3,2,1,0:T(8,128)(2,1)S(1)}, u32[]{:S(2)}, u32[]{:S(2)}) %all-to-all-start.12) | async-done | bytes 2097184 | tf_op jit(solution)/shard_map/all_to_all | solution.py:309
  36.3 112.0 %conditional.1 = (bf16[8,256,256]{2,1,0:T(8,128)(2,1)S(1)}) conditional(s32[]{:T(128)} %bitcast.35, (bf16[8,256,256]{2,1,0:T(8,128)(2,1)}, s32[29]{0:T(128)S(1)}, bf16[8,2,256,256]{3,2,1,0:T(8,128)(2,1)S(1)}) %tuple.77, (bf16[8,256,256]{2,1,0:T(8,128)(2,1)}, s32[29]{0:T(128)S(1)}, ...), branch_computations={%region_0.1_spmd, %region_1.2_spmd, %region_2.3_spmd, %region_3.19... | conditional | flops 3221225472 | bytes 122684160 | solution.py:348
  36.3 1.7 %select.52 = (bf16[2,2,256,256]{3,2,1,0:T(8,128)(2,1)}, bf16[2,2,256,256]{3,2,1,0:T(8,128)(2,1)}) custom-call(s32[29]{0:T(128)S(1)} %get-tuple-element.128.table_ref, bf16[8,2,256,256]{3,2,1,0:T(8,128)(2,1)S(1)} %get-tuple-element.130.own_ref), custom_call_target="tpu_custom_call" | custom-call | bytes 4194304 | tf_op jit(solution)/shard_map/cond/branch_2_fun/select/pallas_call | solution.py:139
  37.9 3.5 %collective-permute-start.28 = (bf16[2,2,256,256]{3,2,1,0:T(8,128)(2,1)}, bf16[2,2,256,256]{3,2,1,0:T(8,128)(2,1)S(1)}, u32[]{:S(2)}, u32[]{:S(2)}) collective-permute-start(bf16[2,2,256,256]{3,2,1,0:T(8,128)(2,1)} %get-tuple-element.131), channel_id=1, source_target_pairs={{0,1},{1,2},{2,3},{4,5},{5,6},{6,7},{8,9},{9,10},{10,11},{12,13},{... | collective-permute-start | bytes 1572872 | tf_op jit(solution)/shard_map/cond/branch_2_fun/ppermute | solution.py:265
  41.5 1.3 collective-permute-start.30
  42.8 3.6 %all-to-all-start.4 = ((bf16[8,256,256]{2,1,0:T(8,128)(2,1)}), bf16[8,256,256]{2,1,0:T(8,128)(2,1)S(1)}, u32[]{:S(2)}, u32[]{:S(2)}) async-start(bf16[8,256,256]{2,1,0:T(8,128)(2,1)} %get-tuple-element.129), calls=%async_computation.4 | async-start | bytes 2097152 | tf_op jit(solution)/shard_map/cond/branch_2_fun/all_to_all | solution.py:309
  46.4 1.9 %select.53 = (bf16[2,2,256,256]{3,2,1,0:T(8,128)(2,1)S(1)}, bf16[2,2,256,256]{3,2,1,0:T(8,128)(2,1)S(1)}) custom-call(s32[29]{0:T(128)S(1)} %get-tuple-element.128.table_ref, bf16[8,2,256,256]{3,2,1,0:T(8,128)(2,1)} %copy-done.9), custom_call_target="tpu_custom_call" | custom-call | bytes 4194304 | tf_op jit(solution)/shard_map/cond/branch_2_fun/select/pallas_call | solution.py:139
  48.2 4.6 %collective-permute-start.29 = (bf16[2,2,256,256]{3,2,1,0:T(8,128)(2,1)S(1)}, bf16[2,2,256,256]{3,2,1,0:T(8,128)(2,1)S(1)}, u32[]{:S(2)}, u32[]{:S(2)}) collective-permute-start(bf16[2,2,256,256]{3,2,1,0:T(8,128)(2,1)S(1)} %get-tuple-element.132), channel_id=1, source_target_pairs={{0,1},{1,2},{2,3},{4,5},{5,6},{6,7},{8,9},{9,10},{10,11},{12,13},{... | collective-permute-start | bytes 1572872 | tf_op jit(solution)/shard_map/cond/branch_2_fun/ppermute | solution.py:265
  52.8 1.3 collective-permute-start.32
  54.2 1.7 %select.54 = (bf16[2,2,256,256]{3,2,1,0:T(8,128)(2,1)}, bf16[2,2,256,256]{3,2,1,0:T(8,128)(2,1)}) custom-call(s32[29]{0:T(128)S(1)} %get-tuple-element.128.table_ref, bf16[8,2,256,256]{3,2,1,0:T(8,128)(2,1)S(1)} %copy-done.10, bf16[2,2,256,256]{3,2,1,0:T(8,128)(2,1)S(1)} %collective-permute-done.28.refs_0_, ...), custom_call_target="tpu_custom_call" | custom-call | bytes 4194304 | tf_op jit(solution)/shard_map/cond/branch_2_fun/select/pallas_call | solution.py:139
  55.8 5.4 %collective-permute-start.31 = (bf16[2,2,256,256]{3,2,1,0:T(8,128)(2,1)}, bf16[2,2,256,256]{3,2,1,0:T(8,128)(2,1)}, u32[]{:S(2)}, u32[]{:S(2)}) collective-permute-start(bf16[2,2,256,256]{3,2,1,0:T(8,128)(2,1)} %get-tuple-element.134), channel_id=1, source_target_pairs={{0,1},{1,2},{2,3},{4,5},{5,6},{6,7},{8,9},{9,10},{10,11},{12,13},{... | collective-permute-start | bytes 1572872 | tf_op jit(solution)/shard_map/cond/branch_2_fun/ppermute | solution.py:265
  62.5 2.5 %collective-permute-done.29.refs_1_ = bf16[2,2,256,256]{3,2,1,0:T(8,128)(2,1)S(1)} collective-permute-done((bf16[2,2,256,256]{3,2,1,0:T(8,128)(2,1)S(1)}, bf16[2,2,256,256]{3,2,1,0:T(8,128)(2,1)S(1)}, u32[]{:S(2)}, u32[]{:S(2)}) %collective-permute-start.29) | collective-permute-done | bytes 524320 | tf_op jit(solution)/shard_map/cond/branch_2_fun/ppermute | solution.py:265
  65.0 4.5 %collective-permute-done.32.refs_3_.refs_4_.refs_5_.refs_6_.refs_7_.refs_8_ = bf16[2,2,256,256]{3,2,1,0:T(8,128)(2,1)S(1)} collective-permute-done((bf16[2,2,256,256]{3,2,1,0:T(8,128)(2,1)S(1)}, bf16[2,2,256,256]{3,2,1,0:T(8,128)(2,1)S(1)}, u32[]{:S(2)}, u32[]{:S(2)}) %collective-permute-start.32) | collective-permute-done | bytes 524320 | tf_op jit(solution)/shard_map/cond/branch_2_fun/ppermute | solution.py:265
  69.5 1.7 %select.55 = (bf16[2,2,256,256]{3,2,1,0:T(8,128)(2,1)}, bf16[2,2,256,256]{3,2,1,0:T(8,128)(2,1)}) custom-call(s32[29]{0:T(128)S(1)} %get-tuple-element.128.table_ref, bf16[8,2,256,256]{3,2,1,0:T(8,128)(2,1)S(1)} %copy-done.10, bf16[2,2,256,256]{3,2,1,0:T(8,128)(2,1)S(1)} %collective-permute-done.28.refs_0_, ...), custom_call_target="tpu_custom_call" | custom-call | bytes 4194304 | tf_op jit(solution)/shard_map/cond/branch_2_fun/select/pallas_call | solution.py:139
  71.2 4.2 %collective-permute-start.33 = (bf16[2,2,256,256]{3,2,1,0:T(8,128)(2,1)}, bf16[2,2,256,256]{3,2,1,0:T(8,128)(2,1)}, u32[]{:S(2)}, u32[]{:S(2)}) collective-permute-start(bf16[2,2,256,256]{3,2,1,0:T(8,128)(2,1)} %get-tuple-element.136), channel_id=1, source_target_pairs={{0,1},{1,2},{2,3},{4,5},{5,6},{6,7},{8,9},{9,10},{10,11},{12,13},{... | collective-permute-start | bytes 1572872 | tf_op jit(solution)/shard_map/cond/branch_2_fun/ppermute | solution.py:265
  76.7 4.1 %collective-permute-done.34.refs_5_.refs_6_.refs_7_.refs_8_.refs_9_ = bf16[2,2,256,256]{3,2,1,0:T(8,128)(2,1)} collective-permute-done((bf16[2,2,256,256]{3,2,1,0:T(8,128)(2,1)}, bf16[2,2,256,256]{3,2,1,0:T(8,128)(2,1)}, u32[]{:S(2)}, u32[]{:S(2)}) %collective-permute-start.34) | collective-permute-done | bytes 524320 | tf_op jit(solution)/shard_map/cond/branch_2_fun/ppermute | solution.py:265
  80.8 1.8 %select.56 = (bf16[2,2,256,256]{3,2,1,0:T(8,128)(2,1)S(1)}, bf16[2,2,256,256]{3,2,1,0:T(8,128)(2,1)S(1)}) custom-call(s32[29]{0:T(128)S(1)} %get-tuple-element.128.table_ref, bf16[8,2,256,256]{3,2,1,0:T(8,128)(2,1)} %copy-done.9, bf16[2,2,256,256]{3,2,1,0:T(8,128)(2,1)S(1)} %collective-permute-done.28.refs_0_, ...), custom_call_target="tpu_custom_call" | custom-call | bytes 4194304 | tf_op jit(solution)/shard_map/cond/branch_2_fun/select/pallas_call | solution.py:139
  82.6 3.5 %collective-permute-start.35 = (bf16[2,2,256,256]{3,2,1,0:T(8,128)(2,1)S(1)}, bf16[2,2,256,256]{3,2,1,0:T(8,128)(2,1)S(1)}, u32[]{:S(2)}, u32[]{:S(2)}) collective-permute-start(bf16[2,2,256,256]{3,2,1,0:T(8,128)(2,1)S(1)} %get-tuple-element.138), channel_id=1, source_target_pairs={{0,1},{1,2},{2,3},{4,5},{5,6},{6,7},{8,9},{9,10},{10,11},{12,13},{... | collective-permute-start | bytes 1572872 | tf_op jit(solution)/shard_map/cond/branch_2_fun/ppermute | solution.py:265
  87.6 4.9 %collective-permute-done.36.refs_7_.refs_8_.refs_9_.refs_10_ = bf16[2,2,256,256]{3,2,1,0:T(8,128)(2,1)} collective-permute-done((bf16[2,2,256,256]{3,2,1,0:T(8,128)(2,1)}, bf16[2,2,256,256]{3,2,1,0:T(8,128)(2,1)}, u32[]{:S(2)}, u32[]{:S(2)}) %collective-permute-start.36) | collective-permute-done | bytes 524320 | tf_op jit(solution)/shard_map/cond/branch_2_fun/ppermute | solution.py:265
  93.2 4.0 %collective-permute-start.37 = (bf16[2,2,256,256]{3,2,1,0:T(8,128)(2,1)S(1)}, bf16[2,2,256,256]{3,2,1,0:T(8,128)(2,1)S(1)}, u32[]{:S(2)}, u32[]{:S(2)}) collective-permute-start(bf16[2,2,256,256]{3,2,1,0:T(8,128)(2,1)S(1)} %get-tuple-element.140), channel_id=1, source_target_pairs={{0,1},{1,2},{2,3},{4,5},{5,6},{6,7},{8,9},{9,10},{10,11},{12,13},{... | collective-permute-start | bytes 1572872 | tf_op jit(solution)/shard_map/cond/branch_2_fun/ppermute | solution.py:265
  97.3 1.3 collective-permute-start.40
  98.7 4.9 %collective-permute-done.38.refs_9_.refs_10_.refs_11_ = bf16[2,2,256,256]{3,2,1,0:T(8,128)(2,1)S(1)} collective-permute-done((bf16[2,2,256,256]{3,2,1,0:T(8,128)(2,1)S(1)}, bf16[2,2,256,256]{3,2,1,0:T(8,128)(2,1)S(1)}, u32[]{:S(2)}, u32[]{:S(2)}) %collective-permute-start.38) | collective-permute-done | bytes 524320 | tf_op jit(solution)/shard_map/cond/branch_2_fun/ppermute | solution.py:265
  104.4 3.1 %collective-permute-start.39 = (bf16[2,2,256,256]{3,2,1,0:T(8,128)(2,1)S(1)}, bf16[2,2,256,256]{3,2,1,0:T(8,128)(2,1)S(1)}, u32[]{:S(2)}, u32[]{:S(2)}) collective-permute-start(bf16[2,2,256,256]{3,2,1,0:T(8,128)(2,1)S(1)} %get-tuple-element.142), channel_id=1, source_target_pairs={{0,1},{1,2},{2,3},{4,5},{5,6},{6,7},{8,9},{9,10},{10,11},{12,13},{... | collective-permute-start | bytes 1572872 | tf_op jit(solution)/shard_map/cond/branch_2_fun/ppermute | solution.py:265
  108.7 4.3 %attend.15.refs_12_ = bf16[8,256,256]{2,1,0:T(8,128)(2,1)S(1)} custom-call(s32[29]{0:T(128)S(1)} %get-tuple-element.128.table_ref, bf16[8,256,256]{2,1,0:T(8,128)(2,1)S(1)} %all-to-all-done.4.refs_6_.q_ref, bf16[8,2,256,256]{3,2,1,0:T(8,128)(2,1)S(1)} %copy-done.11, bf16[2,2,256,256]{3,2,1,0:T(8,128)(2,1)S(1)} %collective-permute-done.28.refs_0_, ...), custom_call_target="tpu_custom_call" | custom-call | flops 1073741824 | bytes 8388608 | tf_op jit(solution)/shard_map/cond/branch_2_fun/attend/pallas_call | solution.py:244
  113.0 1.8 %collective-permute-done.40.refs_11_.refs_12_ = bf16[2,2,256,256]{3,2,1,0:T(8,128)(2,1)S(1)} collective-permute-done((bf16[2,2,256,256]{3,2,1,0:T(8,128)(2,1)S(1)}, bf16[2,2,256,256]{3,2,1,0:T(8,128)(2,1)S(1)}, u32[]{:S(2)}, u32[]{:S(2)}) %collective-permute-start.40) | collective-permute-done | bytes 524320 | tf_op jit(solution)/shard_map/cond/branch_2_fun/ppermute | solution.py:265
  114.8 8.4 %attend.16.refs_14_ = bf16[8,256,256]{2,1,0:T(8,128)(2,1)S(1)} custom-call(s32[29]{0:T(128)S(1)} %get-tuple-element.128.table_ref, bf16[8,256,256]{2,1,0:T(8,128)(2,1)S(1)} %all-to-all-done.4.refs_6_.q_ref, bf16[8,2,256,256]{3,2,1,0:T(8,128)(2,1)S(1)} %copy-done.11, ...), custom_call_target="tpu_custom_call", output_to_operand_aliasing={{}: (15, {})} | custom-call | flops 1073741824 | bytes 8388608 | tf_op jit(solution)/shard_map/cond/branch_2_fun/attend/pallas_call | solution.py:244
  123.2 1.7 %collective-permute-done.41.refs_13_ = bf16[2,2,256,256]{3,2,1,0:T(8,128)(2,1)S(1)} collective-permute-done((bf16[2,2,256,256]{3,2,1,0:T(8,128)(2,1)S(1)}, bf16[2,2,256,256]{3,2,1,0:T(8,128)(2,1)S(1)}, u32[]{:S(2)}, u32[]{:S(2)}) %collective-permute-start.41) | collective-permute-done | bytes 524320 | tf_op jit(solution)/shard_map/cond/branch_2_fun/ppermute | solution.py:265
  124.9 4.3 %attend.17 = bf16[8,256,256]{2,1,0:T(8,128)(2,1)S(1)} custom-call(s32[29]{0:T(128)S(1)} %get-tuple-element.128.table_ref, bf16[8,256,256]{2,1,0:T(8,128)(2,1)S(1)} %all-to-all-done.4.refs_6_.q_ref, bf16[8,2,256,256]{3,2,1,0:T(8,128)(2,1)S(1)} %copy-done.11, ...), custom_call_target="tpu_custom_call", output_to_operand_aliasing={{}: (17, {})} | custom-call | flops 1073741824 | bytes 8388608 | tf_op jit(solution)/shard_map/cond/branch_2_fun/attend/pallas_call | solution.py:244
  129.2 19.0 %all_to_all.55 = bf16[8,256,256]{2,1,0:T(8,128)(2,1)S(1)} all-to-all(bf16[8,256,256]{2,1,0:T(8,128)(2,1)S(1)} %attend.17), channel_id=1, replica_groups=mesh['head'=8,'ctx'=4] {'head'}, dimensions={0} | all-to-all | bytes 2097152 | tf_op jit(solution)/shard_map/cond/branch_2_fun/all_to_all | solution.py:309
  (32 shorter events, 13.1 us)
Async XLA Ops:
  0.0 1.2 copy-start.1
  1.2 1.2 copy-start.2
  4.3 5.3 %copy-start.13 = (s32[16,2]{0,1:T(2,128)S(1)}, s32[16,2]{0,1:T(2,128)}, u32[]{:S(2)}) copy-start(s32[16,2]{0,1:T(2,128)} %param.15) | copy-start | bytes 388
  4.3 10.2 %copy-start = (bf16[256,2048]{1,0:T(8,128)(2,1)S(1)}, bf16[256,2048]{1,0:T(8,128)(2,1)}, u32[]{:S(2)}) copy-start(bf16[256,2048]{1,0:T(8,128)(2,1)} %refs_0_.2) | copy-start | bytes 3145732
  4.3 32.0 %all-to-all-start.12 = ((bf16[8,2,256,256]{3,2,1,0:T(8,128)(2,1)}), bf16[8,2,256,256]{3,2,1,0:T(8,128)(2,1)S(1)}, u32[]{:S(2)}, u32[]{:S(2)}) async-start(bf16[8,2,256,256]{3,2,1,0:T(8,128)(2,1)} %pack.3), calls=%async_computation.12 | async-start | bytes 4194304 | tf_op jit(solution)/shard_map/all_to_all | solution.py:309
  36.3 6.5 %copy-start.9 = (bf16[8,2,256,256]{3,2,1,0:T(8,128)(2,1)}, bf16[8,2,256,256]{3,2,1,0:T(8,128)(2,1)S(1)}, u32[]{:S(2)}) copy-start(bf16[8,2,256,256]{3,2,1,0:T(8,128)(2,1)S(1)} %get-tuple-element.130.own_ref) | copy-start | bytes 6291460 | tf_op jit(solution)/shard_map/cond
  37.9 16.2 %collective-permute-start.28 = (bf16[2,2,256,256]{3,2,1,0:T(8,128)(2,1)}, bf16[2,2,256,256]{3,2,1,0:T(8,128)(2,1)S(1)}, u32[]{:S(2)}, u32[]{:S(2)}) collective-permute-start(bf16[2,2,256,256]{3,2,1,0:T(8,128)(2,1)} %get-tuple-element.131), channel_id=1, source_target_pairs={{0,1},{1,2},{2,3},{4,5},{5,6},{6,7},{8,9},{9,10},{10,11},{12,13},{... | collective-permute-start | bytes 1572872 | tf_op jit(solution)/shard_map/cond/branch_2_fun/ppermute | solution.py:265
  41.5 12.7 %collective-permute-start.30 = (bf16[2,2,256,256]{3,2,1,0:T(8,128)(2,1)}, bf16[2,2,256,256]{3,2,1,0:T(8,128)(2,1)S(1)}, u32[]{:S(2)}, u32[]{:S(2)}) collective-permute-start(bf16[2,2,256,256]{3,2,1,0:T(8,128)(2,1)} %get-tuple-element.133), channel_id=1, source_target_pairs={{1,0},{2,1},{3,2},{5,4},{6,5},{7,6},{9,8},{10,9},{11,10},{13,12},{... | collective-permute-start | bytes 1572872 | tf_op jit(solution)/shard_map/cond/branch_2_fun/ppermute | solution.py:265
  42.8 33.9 %all-to-all-start.4 = ((bf16[8,256,256]{2,1,0:T(8,128)(2,1)}), bf16[8,256,256]{2,1,0:T(8,128)(2,1)S(1)}, u32[]{:S(2)}, u32[]{:S(2)}) async-start(bf16[8,256,256]{2,1,0:T(8,128)(2,1)} %get-tuple-element.129), calls=%async_computation.4 | async-start | bytes 2097152 | tf_op jit(solution)/shard_map/cond/branch_2_fun/all_to_all | solution.py:309
  46.4 7.8 %copy-start.10 = (bf16[8,2,256,256]{3,2,1,0:T(8,128)(2,1)S(1)}, bf16[8,2,256,256]{3,2,1,0:T(8,128)(2,1)}, u32[]{:S(2)}) copy-start(bf16[8,2,256,256]{3,2,1,0:T(8,128)(2,1)} %copy-done.9) | copy-start | bytes 6291460 | tf_op jit(solution)/shard_map/cond
  48.2 16.8 %collective-permute-start.29 = (bf16[2,2,256,256]{3,2,1,0:T(8,128)(2,1)S(1)}, bf16[2,2,256,256]{3,2,1,0:T(8,128)(2,1)S(1)}, u32[]{:S(2)}, u32[]{:S(2)}) collective-permute-start(bf16[2,2,256,256]{3,2,1,0:T(8,128)(2,1)S(1)} %get-tuple-element.132), channel_id=1, source_target_pairs={{0,1},{1,2},{2,3},{4,5},{5,6},{6,7},{8,9},{9,10},{10,11},{12,13},{... | collective-permute-start | bytes 1572872 | tf_op jit(solution)/shard_map/cond/branch_2_fun/ppermute | solution.py:265
  52.8 16.7 %collective-permute-start.32 = (bf16[2,2,256,256]{3,2,1,0:T(8,128)(2,1)S(1)}, bf16[2,2,256,256]{3,2,1,0:T(8,128)(2,1)S(1)}, u32[]{:S(2)}, u32[]{:S(2)}) collective-permute-start(bf16[2,2,256,256]{3,2,1,0:T(8,128)(2,1)S(1)} %get-tuple-element.135), channel_id=1, source_target_pairs={{1,0},{2,1},{3,2},{5,4},{6,5},{7,6},{9,8},{10,9},{11,10},{13,12},{... | collective-permute-start | bytes 1572872 | tf_op jit(solution)/shard_map/cond/branch_2_fun/ppermute | solution.py:265
  55.8 20.9 %collective-permute-start.31 = (bf16[2,2,256,256]{3,2,1,0:T(8,128)(2,1)}, bf16[2,2,256,256]{3,2,1,0:T(8,128)(2,1)}, u32[]{:S(2)}, u32[]{:S(2)}) collective-permute-start(bf16[2,2,256,256]{3,2,1,0:T(8,128)(2,1)} %get-tuple-element.134), channel_id=1, source_target_pairs={{0,1},{1,2},{2,3},{4,5},{5,6},{6,7},{8,9},{9,10},{10,11},{12,13},{... | collective-permute-start | bytes 1572872 | tf_op jit(solution)/shard_map/cond/branch_2_fun/ppermute | solution.py:265
  61.2 19.6 %collective-permute-start.34 = (bf16[2,2,256,256]{3,2,1,0:T(8,128)(2,1)}, bf16[2,2,256,256]{3,2,1,0:T(8,128)(2,1)}, u32[]{:S(2)}, u32[]{:S(2)}) collective-permute-start(bf16[2,2,256,256]{3,2,1,0:T(8,128)(2,1)} %get-tuple-element.137), channel_id=1, source_target_pairs={{1,0},{2,1},{3,2},{5,4},{6,5},{7,6},{9,8},{10,9},{11,10},{13,12},{... | collective-permute-start | bytes 1572872 | tf_op jit(solution)/shard_map/cond/branch_2_fun/ppermute | solution.py:265
  71.2 16.4 %collective-permute-start.33 = (bf16[2,2,256,256]{3,2,1,0:T(8,128)(2,1)}, bf16[2,2,256,256]{3,2,1,0:T(8,128)(2,1)}, u32[]{:S(2)}, u32[]{:S(2)}) collective-permute-start(bf16[2,2,256,256]{3,2,1,0:T(8,128)(2,1)} %get-tuple-element.136), channel_id=1, source_target_pairs={{0,1},{1,2},{2,3},{4,5},{5,6},{6,7},{8,9},{9,10},{10,11},{12,13},{... | collective-permute-start | bytes 1572872 | tf_op jit(solution)/shard_map/cond/branch_2_fun/ppermute | solution.py:265
  75.4 17.1 %collective-permute-start.36 = (bf16[2,2,256,256]{3,2,1,0:T(8,128)(2,1)}, bf16[2,2,256,256]{3,2,1,0:T(8,128)(2,1)}, u32[]{:S(2)}, u32[]{:S(2)}) collective-permute-start(bf16[2,2,256,256]{3,2,1,0:T(8,128)(2,1)} %get-tuple-element.139), channel_id=1, source_target_pairs={{1,0},{2,1},{3,2},{5,4},{6,5},{7,6},{9,8},{10,9},{11,10},{13,12},{... | collective-permute-start | bytes 1572872 | tf_op jit(solution)/shard_map/cond/branch_2_fun/ppermute | solution.py:265
  76.7 15.8 %copy-start.11 = (bf16[8,2,256,256]{3,2,1,0:T(8,128)(2,1)S(1)}, bf16[8,2,256,256]{3,2,1,0:T(8,128)(2,1)}, u32[]{:S(2)}) copy-start(bf16[8,2,256,256]{3,2,1,0:T(8,128)(2,1)} %copy-done.9) | copy-start | bytes 6291460 | tf_op jit(solution)/shard_map/cond
  82.6 16.1 %collective-permute-start.35 = (bf16[2,2,256,256]{3,2,1,0:T(8,128)(2,1)S(1)}, bf16[2,2,256,256]{3,2,1,0:T(8,128)(2,1)S(1)}, u32[]{:S(2)}, u32[]{:S(2)}) collective-permute-start(bf16[2,2,256,256]{3,2,1,0:T(8,128)(2,1)S(1)} %get-tuple-element.138), channel_id=1, source_target_pairs={{0,1},{1,2},{2,3},{4,5},{5,6},{6,7},{8,9},{9,10},{10,11},{12,13},{... | collective-permute-start | bytes 1572872 | tf_op jit(solution)/shard_map/cond/branch_2_fun/ppermute | solution.py:265
  86.1 17.5 %collective-permute-start.38 = (bf16[2,2,256,256]{3,2,1,0:T(8,128)(2,1)S(1)}, bf16[2,2,256,256]{3,2,1,0:T(8,128)(2,1)S(1)}, u32[]{:S(2)}, u32[]{:S(2)}) collective-permute-start(bf16[2,2,256,256]{3,2,1,0:T(8,128)(2,1)S(1)} %get-tuple-element.141), channel_id=1, source_target_pairs={{1,0},{2,1},{3,2},{5,4},{6,5},{7,6},{9,8},{10,9},{11,10},{13,12},{... | collective-permute-start | bytes 1572872 | tf_op jit(solution)/shard_map/cond/branch_2_fun/ppermute | solution.py:265
  93.2 19.8 %collective-permute-start.37 = (bf16[2,2,256,256]{3,2,1,0:T(8,128)(2,1)S(1)}, bf16[2,2,256,256]{3,2,1,0:T(8,128)(2,1)S(1)}, u32[]{:S(2)}, u32[]{:S(2)}) collective-permute-start(bf16[2,2,256,256]{3,2,1,0:T(8,128)(2,1)S(1)} %get-tuple-element.140), channel_id=1, source_target_pairs={{0,1},{1,2},{2,3},{4,5},{5,6},{6,7},{8,9},{9,10},{10,11},{12,13},{... | collective-permute-start | bytes 1572872 | tf_op jit(solution)/shard_map/cond/branch_2_fun/ppermute | solution.py:265
  97.3 17.6 %collective-permute-start.40 = (bf16[2,2,256,256]{3,2,1,0:T(8,128)(2,1)S(1)}, bf16[2,2,256,256]{3,2,1,0:T(8,128)(2,1)S(1)}, u32[]{:S(2)}, u32[]{:S(2)}) collective-permute-start(bf16[2,2,256,256]{3,2,1,0:T(8,128)(2,1)S(1)} %get-tuple-element.143), channel_id=1, source_target_pairs={{1,0},{2,1},{3,2},{5,4},{6,5},{7,6},{9,8},{10,9},{11,10},{13,12},{... | collective-permute-start | bytes 1572872 | tf_op jit(solution)/shard_map/cond/branch_2_fun/ppermute | solution.py:265
  104.4 18.8 %collective-permute-start.39 = (bf16[2,2,256,256]{3,2,1,0:T(8,128)(2,1)S(1)}, bf16[2,2,256,256]{3,2,1,0:T(8,128)(2,1)S(1)}, u32[]{:S(2)}, u32[]{:S(2)}) collective-permute-start(bf16[2,2,256,256]{3,2,1,0:T(8,128)(2,1)S(1)} %get-tuple-element.142), channel_id=1, source_target_pairs={{0,1},{1,2},{2,3},{4,5},{5,6},{6,7},{8,9},{9,10},{10,11},{12,13},{... | collective-permute-start | bytes 1572872 | tf_op jit(solution)/shard_map/cond/branch_2_fun/ppermute | solution.py:265
  107.4 17.5 %collective-permute-start.41 = (bf16[2,2,256,256]{3,2,1,0:T(8,128)(2,1)S(1)}, bf16[2,2,256,256]{3,2,1,0:T(8,128)(2,1)S(1)}, u32[]{:S(2)}, u32[]{:S(2)}) collective-permute-start(bf16[2,2,256,256]{3,2,1,0:T(8,128)(2,1)S(1)} %get-tuple-element.144), channel_id=1, source_target_pairs={{1,0},{2,1},{3,2},{5,4},{6,5},{7,6},{9,8},{10,9},{11,10},{13,12},{... | collective-permute-start | bytes 1572872 | tf_op jit(solution)/shard_map/cond/branch_2_fun/ppermute | solution.py:265

commit v2 on v1

--- a/solution.py
+++ b/solution.py
@@ -300,7 +300,7 @@
             pltpu.SemaphoreType.DMA((head_count, len(arrays))),
             pltpu.SemaphoreType.DMA((head_count,)),
         ],
-        compiler_params=pltpu.CompilerParams(vmem_limit_bytes=8 << 20),
+        compiler_params=pltpu.CompilerParams(vmem_limit_bytes=60 << 20),
         name="pack",
     )(*arrays)
 

time: 149 us -> 136 us (0.913); the launches traced: 149 us -> 134 us
  waiting for transfers between devices: 45.3 us -> 35.4 us
  starting transfers between devices: 46.1 us -> 41.6 us
  local copies, waits for them, and re-layouts: 4.83 us -> 2.38 us
    ppermute x14 -> x12, waiting for transfers between devices: 24.7 us -> 15.7 us  [shift(): return lax.ppermute(x, 'ctx', pairs)]
    ppermute x14 -> x12, starting transfers between devices: 37.3 us -> 32.9 us  [shift(): return lax.ppermute(x, 'ctx', pairs)]
    unnamed x9 -> x3, local copies, waits for them, and re-layouts: 3.14 us -> 0.69 us
    pallas_call x2, Pallas kernels: 3.08 us -> 4.68 us  [pack(): pl.pallas_call(functools.partial(pack_kernel, head_count), out_shape=jax....]
    pallas_call x7 -> x6, Pallas kernels: 10.1 us -> 10.1 us  [select(): pl.pallas_call(functools.partial(select_kernel, t, local_blocks, parts, c...]
  transfers between devices with their start and end apart: 16 -> 14, of which waited for: 10 -> 8; matrix products, arithmetic and copies ran while one was open for 1% -> 1% of each run, Pallas kernels for 17% -> 18%
where the time goes in v2:
time: 136 us; the launch traced here: 134 us
  starting transfers between devices  41.6 us (31%)
  waiting for transfers between devices  35.4 us (26%)
  Pallas kernels  33.2 us (24%)
  blocking collectives  19.7 us (14%)
  local copies, waits for them, and re-layouts  2.38 us (2%)
    ppermute x12, starting transfers between devices, shift(): return lax.ppermute(x, 'ctx', pairs)  32.9 us
    all_to_all x1, blocking collectives, swap(): return lax.all_to_all(x, 'head', split_axis=0, concat_axis=0, tiled=True)  19.7 us
    all_to_all x2, waiting for transfers between devices, swap(): return lax.all_to_all(x, 'head', split_axis=0, concat_axis=0, tiled=True)  19.7 us
    pallas_call x3, Pallas kernels, attend(): pl.pallas_call(functools.partial(attend_kernel, low, high, local_blocks,...  16.2 us
    ppermute x12, waiting for transfers between devices, shift(): return lax.ppermute(x, 'ctx', pairs)  15.7 us
    pallas_call x6, Pallas kernels, select(): pl.pallas_call(functools.partial(select_kernel, t, local_blocks, parts, c...  10.1 us
    all_to_all x2, starting transfers between devices, swap(): return lax.all_to_all(x, 'head', split_axis=0, concat_axis=0, tiled=True)  8.75 us
    pallas_call x2, Pallas kernels, pack(): pl.pallas_call(functools.partial(pack_kernel, head_count), out_shape=jax....  4.68 us
  transfers between devices with their start and end apart: 14, of which 8 were waited for; matrix products, arithmetic and copies ran while one was open for 1% of the time, Pallas kernels for 18%

profile of v2, /device:TPU:0, one launch (start us, length us, event | category | flops | bytes accessed | tf_op | source)
XLA Modules:
  0.0 133.9 jit_solution(4267385829168595521)
XLA Ops:
  0.0 2.6 %pack.3 = bf16[8,2,256,256]{3,2,1,0:T(8,128)(2,1)} custom-call(bf16[256,2048]{1,0:T(8,128)(2,1)} %refs_0_.3, bf16[256,2048]{1,0:T(8,128)(2,1)} %refs_1_.1), custom_call_target="tpu_custom_call" | custom-call | tf_op jit(solution)/shard_map/pack/pallas_call | solution.py:293
  2.6 5.2 %all-to-all-start.12 = ((bf16[8,2,256,256]{3,2,1,0:T(8,128)(2,1)}), bf16[8,2,256,256]{3,2,1,0:T(8,128)(2,1)S(1)}, u32[]{:S(2)}, u32[]{:S(2)}) async-start(bf16[8,2,256,256]{3,2,1,0:T(8,128)(2,1)} %pack.3), calls=%async_computation.12 | async-start | bytes 4194304 | tf_op jit(solution)/shard_map/all_to_all | solution.py:309
  8.5 2.3 %plan.1 = s32[29]{0:T(128)S(1)} custom-call(s32[1]{0:T(128)} %bitcast.34.me_ref, s32[16,2]{1,0:T(8,128)} %copy.41.picks_ref), custom_call_target="tpu_custom_call" | custom-call | tf_op jit(solution)/shard_map/plan/pallas_call | solution.py:101
  12.7 2.1 %pack.2 = bf16[8,1,256,256]{3,2,1,0:T(8,128)(2,1)} custom-call(bf16[256,2048]{1,0:T(8,128)(2,1)} %refs_0_.2), custom_call_target="tpu_custom_call" | custom-call | tf_op jit(solution)/shard_map/pack/pallas_call | solution.py:293
  14.8 19.7 %all-to-all-done.12 = bf16[8,2,256,256]{3,2,1,0:T(8,128)(2,1)S(1)} async-done(((bf16[8,2,256,256]{3,2,1,0:T(8,128)(2,1)}), bf16[8,2,256,256]{3,2,1,0:T(8,128)(2,1)S(1)}, u32[]{:S(2)}, u32[]{:S(2)}) %all-to-all-start.12) | async-done | bytes 2097184 | tf_op jit(solution)/shard_map/all_to_all | solution.py:309
  34.4 98.3 %conditional.1 = (bf16[8,256,256]{2,1,0:T(8,128)(2,1)S(1)}) conditional(s32[]{:T(128)} %bitcast.35, (bf16[8,256,256]{2,1,0:T(8,128)(2,1)}, s32[29]{0:T(128)S(1)}, bf16[8,2,256,256]{3,2,1,0:T(8,128)(2,1)S(1)}) %tuple.77, (bf16[8,256,256]{2,1,0:T(8,128)(2,1)}, s32[29]{0:T(128)S(1)}, ...), branch_computations={%region_0.1_spmd, %region_1.2_spmd, %region_2.3_spmd, %region_3.19... | conditional | flops 3221225472 | bytes 122684160 | solution.py:348
  34.4 1.6 %select.46 = (bf16[2,2,256,256]{3,2,1,0:T(8,128)(2,1)}, bf16[2,2,256,256]{3,2,1,0:T(8,128)(2,1)}) custom-call(s32[29]{0:T(128)S(1)} %get-tuple-element.113.table_ref, bf16[8,2,256,256]{3,2,1,0:T(8,128)(2,1)S(1)} %get-tuple-element.115.own_ref), custom_call_target="tpu_custom_call" | custom-call | bytes 4194304 | tf_op jit(solution)/shard_map/cond/branch_1_fun/select/pallas_call | solution.py:139
  36.1 3.5 %collective-permute-start.16 = (bf16[2,2,256,256]{3,2,1,0:T(8,128)(2,1)}, bf16[2,2,256,256]{3,2,1,0:T(8,128)(2,1)S(1)}, u32[]{:S(2)}, u32[]{:S(2)}) collective-permute-start(bf16[2,2,256,256]{3,2,1,0:T(8,128)(2,1)} %get-tuple-element.116), channel_id=1, source_target_pairs={{0,1},{1,2},{2,3},{4,5},{5,6},{6,7},{8,9},{9,10},{10,11},{12,13},{... | collective-permute-start | bytes 1572872 | tf_op jit(solution)/shard_map/cond/branch_1_fun/ppermute | solution.py:265
  39.6 1.3 collective-permute-start.18
  40.9 1.7 %select.47 = (bf16[2,2,256,256]{3,2,1,0:T(8,128)(2,1)}, bf16[2,2,256,256]{3,2,1,0:T(8,128)(2,1)}) custom-call(s32[29]{0:T(128)S(1)} %get-tuple-element.113.table_ref, bf16[8,2,256,256]{3,2,1,0:T(8,128)(2,1)S(1)} %get-tuple-element.115.own_ref), custom_call_target="tpu_custom_call" | custom-call | bytes 4194304 | tf_op jit(solution)/shard_map/cond/branch_1_fun/select/pallas_call | solution.py:139
  42.6 4.6 %collective-permute-start.17 = (bf16[2,2,256,256]{3,2,1,0:T(8,128)(2,1)}, bf16[2,2,256,256]{3,2,1,0:T(8,128)(2,1)S(1)}, u32[]{:S(2)}, u32[]{:S(2)}) collective-permute-start(bf16[2,2,256,256]{3,2,1,0:T(8,128)(2,1)} %get-tuple-element.117), channel_id=1, source_target_pairs={{0,1},{1,2},{2,3},{4,5},{5,6},{6,7},{8,9},{9,10},{10,11},{12,13},{... | collective-permute-start | bytes 1572872 | tf_op jit(solution)/shard_map/cond/branch_1_fun/ppermute | solution.py:265
  47.2 1.3 collective-permute-start.20
  48.5 3.6 %all-to-all-start.2 = ((bf16[8,256,256]{2,1,0:T(8,128)(2,1)}), bf16[8,256,256]{2,1,0:T(8,128)(2,1)S(1)}, u32[]{:S(2)}, u32[]{:S(2)}) async-start(bf16[8,256,256]{2,1,0:T(8,128)(2,1)} %get-tuple-element.114), calls=%async_computation.2 | async-start | bytes 2097152 | tf_op jit(solution)/shard_map/cond/branch_1_fun/all_to_all | solution.py:309
  52.3 4.2 %collective-permute-done.18.refs_1_.refs_2_.refs_3_.refs_4_.refs_5_.refs_6_ = bf16[2,2,256,256]{3,2,1,0:T(8,128)(2,1)S(1)} collective-permute-done((bf16[2,2,256,256]{3,2,1,0:T(8,128)(2,1)}, bf16[2,2,256,256]{3,2,1,0:T(8,128)(2,1)S(1)}, u32[]{:S(2)}, u32[]{:S(2)}) %collective-permute-start.18) | collective-permute-done | bytes 524320 | tf_op jit(solution)/shard_map/cond/branch_1_fun/ppermute | solution.py:265
  56.5 2.6 %select.48 = (bf16[2,2,256,256]{3,2,1,0:T(8,128)(2,1)}, bf16[2,2,256,256]{3,2,1,0:T(8,128)(2,1)}) custom-call(s32[29]{0:T(128)S(1)} %get-tuple-element.113.table_ref, bf16[8,2,256,256]{3,2,1,0:T(8,128)(2,1)} %copy-done.3, bf16[2,2,256,256]{3,2,1,0:T(8,128)(2,1)S(1)} %collective-permute-done.16.refs_0_, ...), custom_call_target="tpu_custom_call" | custom-call | bytes 4194304 | tf_op jit(solution)/shard_map/cond/branch_1_fun/select/pallas_call | solution.py:139
  59.1 3.3 %collective-permute-start.19 = (bf16[2,2,256,256]{3,2,1,0:T(8,128)(2,1)}, bf16[2,2,256,256]{3,2,1,0:T(8,128)(2,1)}, u32[]{:S(2)}, u32[]{:S(2)}) collective-permute-start(bf16[2,2,256,256]{3,2,1,0:T(8,128)(2,1)} %get-tuple-element.119), channel_id=1, source_target_pairs={{0,1},{1,2},{2,3},{4,5},{5,6},{6,7},{8,9},{9,10},{10,11},{12,13},{... | collective-permute-start | bytes 1572872 | tf_op jit(solution)/shard_map/cond/branch_1_fun/ppermute | solution.py:265
  62.4 1.3 collective-permute-start.22
  63.7 1.7 %select.49 = (bf16[2,2,256,256]{3,2,1,0:T(8,128)(2,1)}, bf16[2,2,256,256]{3,2,1,0:T(8,128)(2,1)}) custom-call(s32[29]{0:T(128)S(1)} %get-tuple-element.113.table_ref, bf16[8,2,256,256]{3,2,1,0:T(8,128)(2,1)S(1)} %copy-done.4, bf16[2,2,256,256]{3,2,1,0:T(8,128)(2,1)S(1)} %collective-permute-done.16.refs_0_, ...), custom_call_target="tpu_custom_call" | custom-call | bytes 4194304 | tf_op jit(solution)/shard_map/cond/branch_1_fun/select/pallas_call | solution.py:139
  65.4 5.4 %collective-permute-start.21 = (bf16[2,2,256,256]{3,2,1,0:T(8,128)(2,1)}, bf16[2,2,256,256]{3,2,1,0:T(8,128)(2,1)}, u32[]{:S(2)}, u32[]{:S(2)}) collective-permute-start(bf16[2,2,256,256]{3,2,1,0:T(8,128)(2,1)} %get-tuple-element.121), channel_id=1, source_target_pairs={{0,1},{1,2},{2,3},{4,5},{5,6},{6,7},{8,9},{9,10},{10,11},{12,13},{... | collective-permute-start | bytes 1572872 | tf_op jit(solution)/shard_map/cond/branch_1_fun/ppermute | solution.py:265
  70.7 1.3 collective-permute-start.24
  72.0 2.2 %collective-permute-done.19.refs_2_ = bf16[2,2,256,256]{3,2,1,0:T(8,128)(2,1)} collective-permute-done((bf16[2,2,256,256]{3,2,1,0:T(8,128)(2,1)}, bf16[2,2,256,256]{3,2,1,0:T(8,128)(2,1)}, u32[]{:S(2)}, u32[]{:S(2)}) %collective-permute-start.19) | collective-permute-done | bytes 524320 | tf_op jit(solution)/shard_map/cond/branch_1_fun/ppermute | solution.py:265
  74.3 4.3 %collective-permute-done.22.refs_5_.refs_6_.refs_7_.refs_8_ = bf16[2,2,256,256]{3,2,1,0:T(8,128)(2,1)} collective-permute-done((bf16[2,2,256,256]{3,2,1,0:T(8,128)(2,1)}, bf16[2,2,256,256]{3,2,1,0:T(8,128)(2,1)}, u32[]{:S(2)}, u32[]{:S(2)}) %collective-permute-start.22) | collective-permute-done | bytes 524320 | tf_op jit(solution)/shard_map/cond/branch_1_fun/ppermute | solution.py:265
  78.5 1.8 %select.50 = (bf16[2,2,256,256]{3,2,1,0:T(8,128)(2,1)S(1)}, bf16[2,2,256,256]{3,2,1,0:T(8,128)(2,1)S(1)}) custom-call(s32[29]{0:T(128)S(1)} %get-tuple-element.113.table_ref, bf16[8,2,256,256]{3,2,1,0:T(8,128)(2,1)} %copy-done.3, bf16[2,2,256,256]{3,2,1,0:T(8,128)(2,1)S(1)} %collective-permute-done.16.refs_0_, ...), custom_call_target="tpu_custom_call" | custom-call | bytes 4194304 | tf_op jit(solution)/shard_map/cond/branch_1_fun/select/pallas_call | solution.py:139
  80.3 3.6 %collective-permute-start.23 = (bf16[2,2,256,256]{3,2,1,0:T(8,128)(2,1)S(1)}, bf16[2,2,256,256]{3,2,1,0:T(8,128)(2,1)S(1)}, u32[]{:S(2)}, u32[]{:S(2)}) collective-permute-start(bf16[2,2,256,256]{3,2,1,0:T(8,128)(2,1)S(1)} %get-tuple-element.123), channel_id=1, source_target_pairs={{0,1},{1,2},{2,3},{4,5},{5,6},{6,7},{8,9},{9,10},{10,11},{12,13},{... | collective-permute-start | bytes 1572872 | tf_op jit(solution)/shard_map/cond/branch_1_fun/ppermute | solution.py:265
  84.0 1.3 collective-permute-start.26
  85.5 4.3 %collective-permute-done.24.refs_7_.refs_8_.refs_9_ = bf16[2,2,256,256]{3,2,1,0:T(8,128)(2,1)} collective-permute-done((bf16[2,2,256,256]{3,2,1,0:T(8,128)(2,1)}, bf16[2,2,256,256]{3,2,1,0:T(8,128)(2,1)}, u32[]{:S(2)}, u32[]{:S(2)}) %collective-permute-start.24) | collective-permute-done | bytes 524320 | tf_op jit(solution)/shard_map/cond/branch_1_fun/ppermute | solution.py:265
  90.5 4.6 %collective-permute-start.25 = (bf16[2,2,256,256]{3,2,1,0:T(8,128)(2,1)S(1)}, bf16[2,2,256,256]{3,2,1,0:T(8,128)(2,1)S(1)}, u32[]{:S(2)}, u32[]{:S(2)}) collective-permute-start(bf16[2,2,256,256]{3,2,1,0:T(8,128)(2,1)S(1)} %get-tuple-element.125), channel_id=1, source_target_pairs={{0,1},{1,2},{2,3},{4,5},{5,6},{6,7},{8,9},{9,10},{10,11},{12,13},{... | collective-permute-start | bytes 1572872 | tf_op jit(solution)/shard_map/cond/branch_1_fun/ppermute | solution.py:265
  95.1 1.5 %collective-permute-start.27 = (bf16[2,2,256,256]{3,2,1,0:T(8,128)(2,1)S(1)}, bf16[2,2,256,256]{3,2,1,0:T(8,128)(2,1)S(1)}, u32[]{:S(2)}, u32[]{:S(2)}) collective-permute-start(bf16[2,2,256,256]{3,2,1,0:T(8,128)(2,1)S(1)} %get-tuple-element.127), channel_id=1, source_target_pairs={{1,0},{2,1},{3,2},{5,4},{6,5},{7,6},{9,8},{10,9},{11,10},{13,12},{... | collective-permute-start | bytes 1572872 | tf_op jit(solution)/shard_map/cond/branch_1_fun/ppermute | solution.py:265
  96.6 4.3 %attend.12.refs_10_ = bf16[8,256,256]{2,1,0:T(8,128)(2,1)S(1)} custom-call(s32[29]{0:T(128)S(1)} %get-tuple-element.113.table_ref, bf16[8,256,256]{2,1,0:T(8,128)(2,1)S(1)} %all-to-all-done.2.refs_6_.q_ref, bf16[8,2,256,256]{3,2,1,0:T(8,128)(2,1)S(1)} %copy-done.5, bf16[2,2,256,256]{3,2,1,0:T(8,128)(2,1)S(1)} %collective-permute-done.16.refs_0_, ...), custom_call_target="tpu_custom_call" | custom-call | flops 1073741824 | bytes 8388608 | tf_op jit(solution)/shard_map/cond/branch_1_fun/attend/pallas_call | solution.py:244
  100.9 7.6 %attend.13.refs_12_ = bf16[8,256,256]{2,1,0:T(8,128)(2,1)S(1)} custom-call(s32[29]{0:T(128)S(1)} %get-tuple-element.113.table_ref, bf16[8,256,256]{2,1,0:T(8,128)(2,1)S(1)} %all-to-all-done.2.refs_6_.q_ref, bf16[8,2,256,256]{3,2,1,0:T(8,128)(2,1)S(1)} %copy-done.5, ...), custom_call_target="tpu_custom_call", output_to_operand_aliasing={{}: (13, {})} | custom-call | flops 1073741824 | bytes 8388608 | tf_op jit(solution)/shard_map/cond/branch_1_fun/attend/pallas_call | solution.py:244
  108.8 4.3 %attend.14 = bf16[8,256,256]{2,1,0:T(8,128)(2,1)S(1)} custom-call(s32[29]{0:T(128)S(1)} %get-tuple-element.113.table_ref, bf16[8,256,256]{2,1,0:T(8,128)(2,1)S(1)} %all-to-all-done.2.refs_6_.q_ref, bf16[8,2,256,256]{3,2,1,0:T(8,128)(2,1)S(1)} %copy-done.5, ...), custom_call_target="tpu_custom_call", output_to_operand_aliasing={{}: (15, {})} | custom-call | flops 1073741824 | bytes 8388608 | tf_op jit(solution)/shard_map/cond/branch_1_fun/attend/pallas_call | solution.py:244
  113.1 19.7 %all_to_all.54 = bf16[8,256,256]{2,1,0:T(8,128)(2,1)S(1)} all-to-all(bf16[8,256,256]{2,1,0:T(8,128)(2,1)S(1)} %attend.14), channel_id=1, replica_groups=mesh['head'=8,'ctx'=4] {'head'}, dimensions={0} | all-to-all | bytes 2097152 | tf_op jit(solution)/shard_map/cond/branch_1_fun/all_to_all | solution.py:309
  (21 shorter events, 3.8 us)
Async XLA Ops:
  2.6 5.2 %copy-start.10 = (s32[16,2]{0,1:T(2,128)S(1)}, s32[16,2]{0,1:T(2,128)}, u32[]{:S(2)}) copy-start(s32[16,2]{0,1:T(2,128)} %param.15) | copy-start | bytes 388
  2.6 31.8 %all-to-all-start.12 = ((bf16[8,2,256,256]{3,2,1,0:T(8,128)(2,1)}), bf16[8,2,256,256]{3,2,1,0:T(8,128)(2,1)S(1)}, u32[]{:S(2)}, u32[]{:S(2)}) async-start(bf16[8,2,256,256]{3,2,1,0:T(8,128)(2,1)} %pack.3), calls=%async_computation.12 | async-start | bytes 4194304 | tf_op jit(solution)/shard_map/all_to_all | solution.py:309
  34.4 8.1 %copy-start.3 = (bf16[8,2,256,256]{3,2,1,0:T(8,128)(2,1)}, bf16[8,2,256,256]{3,2,1,0:T(8,128)(2,1)S(1)}, u32[]{:S(2)}) copy-start(bf16[8,2,256,256]{3,2,1,0:T(8,128)(2,1)S(1)} %get-tuple-element.115.own_ref) | copy-start | bytes 6291460 | tf_op jit(solution)/shard_map/cond
  36.1 16.2 %collective-permute-start.16 = (bf16[2,2,256,256]{3,2,1,0:T(8,128)(2,1)}, bf16[2,2,256,256]{3,2,1,0:T(8,128)(2,1)S(1)}, u32[]{:S(2)}, u32[]{:S(2)}) collective-permute-start(bf16[2,2,256,256]{3,2,1,0:T(8,128)(2,1)} %get-tuple-element.116), channel_id=1, source_target_pairs={{0,1},{1,2},{2,3},{4,5},{5,6},{6,7},{8,9},{9,10},{10,11},{12,13},{... | collective-permute-start | bytes 1572872 | tf_op jit(solution)/shard_map/cond/branch_1_fun/ppermute | solution.py:265
  39.6 16.9 %collective-permute-start.18 = (bf16[2,2,256,256]{3,2,1,0:T(8,128)(2,1)}, bf16[2,2,256,256]{3,2,1,0:T(8,128)(2,1)S(1)}, u32[]{:S(2)}, u32[]{:S(2)}) collective-permute-start(bf16[2,2,256,256]{3,2,1,0:T(8,128)(2,1)} %get-tuple-element.118), channel_id=1, source_target_pairs={{1,0},{2,1},{3,2},{5,4},{6,5},{7,6},{9,8},{10,9},{11,10},{13,12},{... | collective-permute-start | bytes 1572872 | tf_op jit(solution)/shard_map/cond/branch_1_fun/ppermute | solution.py:265
  42.6 21.1 %collective-permute-start.17 = (bf16[2,2,256,256]{3,2,1,0:T(8,128)(2,1)}, bf16[2,2,256,256]{3,2,1,0:T(8,128)(2,1)S(1)}, u32[]{:S(2)}, u32[]{:S(2)}) collective-permute-start(bf16[2,2,256,256]{3,2,1,0:T(8,128)(2,1)} %get-tuple-element.117), channel_id=1, source_target_pairs={{0,1},{1,2},{2,3},{4,5},{5,6},{6,7},{8,9},{9,10},{10,11},{12,13},{... | collective-permute-start | bytes 1572872 | tf_op jit(solution)/shard_map/cond/branch_1_fun/ppermute | solution.py:265
  47.2 16.5 %collective-permute-start.20 = (bf16[2,2,256,256]{3,2,1,0:T(8,128)(2,1)}, bf16[2,2,256,256]{3,2,1,0:T(8,128)(2,1)S(1)}, u32[]{:S(2)}, u32[]{:S(2)}) collective-permute-start(bf16[2,2,256,256]{3,2,1,0:T(8,128)(2,1)} %get-tuple-element.120), channel_id=1, source_target_pairs={{1,0},{2,1},{3,2},{5,4},{6,5},{7,6},{9,8},{10,9},{11,10},{13,12},{... | collective-permute-start | bytes 1572872 | tf_op jit(solution)/shard_map/cond/branch_1_fun/ppermute | solution.py:265
  48.5 23.6 %all-to-all-start.2 = ((bf16[8,256,256]{2,1,0:T(8,128)(2,1)}), bf16[8,256,256]{2,1,0:T(8,128)(2,1)S(1)}, u32[]{:S(2)}, u32[]{:S(2)}) async-start(bf16[8,256,256]{2,1,0:T(8,128)(2,1)} %get-tuple-element.114), calls=%async_computation.2 | async-start | bytes 2097152 | tf_op jit(solution)/shard_map/cond/branch_1_fun/all_to_all | solution.py:309
  52.0 11.6 %copy-start.4 = (bf16[8,2,256,256]{3,2,1,0:T(8,128)(2,1)S(1)}, bf16[8,2,256,256]{3,2,1,0:T(8,128)(2,1)}, u32[]{:S(2)}) copy-start(bf16[8,2,256,256]{3,2,1,0:T(8,128)(2,1)} %copy-done.3) | copy-start | bytes 6291460 | tf_op jit(solution)/shard_map/cond
  59.1 15.2 %collective-permute-start.19 = (bf16[2,2,256,256]{3,2,1,0:T(8,128)(2,1)}, bf16[2,2,256,256]{3,2,1,0:T(8,128)(2,1)}, u32[]{:S(2)}, u32[]{:S(2)}) collective-permute-start(bf16[2,2,256,256]{3,2,1,0:T(8,128)(2,1)} %get-tuple-element.119), channel_id=1, source_target_pairs={{0,1},{1,2},{2,3},{4,5},{5,6},{6,7},{8,9},{9,10},{10,11},{12,13},{... | collective-permute-start | bytes 1572872 | tf_op jit(solution)/shard_map/cond/branch_1_fun/ppermute | solution.py:265
  62.4 16.2 %collective-permute-start.22 = (bf16[2,2,256,256]{3,2,1,0:T(8,128)(2,1)}, bf16[2,2,256,256]{3,2,1,0:T(8,128)(2,1)}, u32[]{:S(2)}, u32[]{:S(2)}) collective-permute-start(bf16[2,2,256,256]{3,2,1,0:T(8,128)(2,1)} %get-tuple-element.122), channel_id=1, source_target_pairs={{1,0},{2,1},{3,2},{5,4},{6,5},{7,6},{9,8},{10,9},{11,10},{13,12},{... | collective-permute-start | bytes 1572872 | tf_op jit(solution)/shard_map/cond/branch_1_fun/ppermute | solution.py:265
  65.4 20.1 %collective-permute-start.21 = (bf16[2,2,256,256]{3,2,1,0:T(8,128)(2,1)}, bf16[2,2,256,256]{3,2,1,0:T(8,128)(2,1)}, u32[]{:S(2)}, u32[]{:S(2)}) collective-permute-start(bf16[2,2,256,256]{3,2,1,0:T(8,128)(2,1)} %get-tuple-element.121), channel_id=1, source_target_pairs={{0,1},{1,2},{2,3},{4,5},{5,6},{6,7},{8,9},{9,10},{10,11},{12,13},{... | collective-permute-start | bytes 1572872 | tf_op jit(solution)/shard_map/cond/branch_1_fun/ppermute | solution.py:265
  70.7 19.0 %collective-permute-start.24 = (bf16[2,2,256,256]{3,2,1,0:T(8,128)(2,1)}, bf16[2,2,256,256]{3,2,1,0:T(8,128)(2,1)}, u32[]{:S(2)}, u32[]{:S(2)}) collective-permute-start(bf16[2,2,256,256]{3,2,1,0:T(8,128)(2,1)} %get-tuple-element.124), channel_id=1, source_target_pairs={{1,0},{2,1},{3,2},{5,4},{6,5},{7,6},{9,8},{10,9},{11,10},{13,12},{... | collective-permute-start | bytes 1572872 | tf_op jit(solution)/shard_map/cond/branch_1_fun/ppermute | solution.py:265
  72.0 17.8 %copy-start.5 = (bf16[8,2,256,256]{3,2,1,0:T(8,128)(2,1)S(1)}, bf16[8,2,256,256]{3,2,1,0:T(8,128)(2,1)}, u32[]{:S(2)}) copy-start(bf16[8,2,256,256]{3,2,1,0:T(8,128)(2,1)} %copy-done.3) | copy-start | bytes 6291460 | tf_op jit(solution)/shard_map/cond
  80.3 20.5 %collective-permute-start.23 = (bf16[2,2,256,256]{3,2,1,0:T(8,128)(2,1)S(1)}, bf16[2,2,256,256]{3,2,1,0:T(8,128)(2,1)S(1)}, u32[]{:S(2)}, u32[]{:S(2)}) collective-permute-start(bf16[2,2,256,256]{3,2,1,0:T(8,128)(2,1)S(1)} %get-tuple-element.123), channel_id=1, source_target_pairs={{0,1},{1,2},{2,3},{4,5},{5,6},{6,7},{8,9},{9,10},{10,11},{12,13},{... | collective-permute-start | bytes 1572872 | tf_op jit(solution)/shard_map/cond/branch_1_fun/ppermute | solution.py:265
  84.0 16.9 %collective-permute-start.26 = (bf16[2,2,256,256]{3,2,1,0:T(8,128)(2,1)S(1)}, bf16[2,2,256,256]{3,2,1,0:T(8,128)(2,1)S(1)}, u32[]{:S(2)}, u32[]{:S(2)}) collective-permute-start(bf16[2,2,256,256]{3,2,1,0:T(8,128)(2,1)S(1)} %get-tuple-element.126), channel_id=1, source_target_pairs={{1,0},{2,1},{3,2},{5,4},{6,5},{7,6},{9,8},{10,9},{11,10},{13,12},{... | collective-permute-start | bytes 1572872 | tf_op jit(solution)/shard_map/cond/branch_1_fun/ppermute | solution.py:265
  90.5 18.0 %collective-permute-start.25 = (bf16[2,2,256,256]{3,2,1,0:T(8,128)(2,1)S(1)}, bf16[2,2,256,256]{3,2,1,0:T(8,128)(2,1)S(1)}, u32[]{:S(2)}, u32[]{:S(2)}) collective-permute-start(bf16[2,2,256,256]{3,2,1,0:T(8,128)(2,1)S(1)} %get-tuple-element.125), channel_id=1, source_target_pairs={{0,1},{1,2},{2,3},{4,5},{5,6},{6,7},{8,9},{9,10},{10,11},{12,13},{... | collective-permute-start | bytes 1572872 | tf_op jit(solution)/shard_map/cond/branch_1_fun/ppermute | solution.py:265
  95.1 13.7 %collective-permute-start.27 = (bf16[2,2,256,256]{3,2,1,0:T(8,128)(2,1)S(1)}, bf16[2,2,256,256]{3,2,1,0:T(8,128)(2,1)S(1)}, u32[]{:S(2)}, u32[]{:S(2)}) collective-permute-start(bf16[2,2,256,256]{3,2,1,0:T(8,128)(2,1)S(1)} %get-tuple-element.127), channel_id=1, source_target_pairs={{1,0},{2,1},{3,2},{5,4},{6,5},{7,6},{9,8},{10,9},{11,10},{13,12},{... | collective-permute-start | bytes 1572872 | tf_op jit(solution)/shard_map/cond/branch_1_fun/ppermute | solution.py:265
